TPU v7x, 128 devices: a whole 4x4x4 slice. The times are simulated.
128 devices in a mesh: group: 4 (over x_lo, core), tensor: 32 (over x_hi, y, z).
Axes of the slice: x: 4 (x_hi: 2, x_lo: 2; x = x_hi * 2 + x_lo), y: 4, z: 4, core: 2. Of those that a mesh axis runs over, the one named last changes fastest.
Arguments:
- tokens: bfloat16 [512, 3, 8192], P(('group', 'tensor')), may hold values from -6 to 6
- norm_gain: float32 [8192], replicated, may hold values from 0.25 to 1.75
- w_qkv: bfloat16 [8192, 10240], P(None, 'tensor'), may hold values from -0.0625 to 0.0625
- w_out: bfloat16 [8192, 8192], P('tensor'), may hold values from -0.0625 to 0.0625
- lengths: int32 [128, 4], P(('group', 'tensor')), may hold values from 1 to 512, 1024 in all within a row
- migrate: int32 [128, 4], P(('group', 'tensor')), may hold values from 0 to 3, as said below
- page_order: int32 [128, 12], P(('group', 'tensor')), may hold values from 0 to 11, each once within a row
- kv_pool: bfloat16 [128, 12, 2, 8, 128, 128], P(('group', 'tensor')), as said below
Outputs:
- mixed: bfloat16 [512, 3, 8192], P(('group', 'tensor'))
Inputs may be any that keep to these rules, and one draw needn't show every extreme that they name: `migrate`: on each device every group number is named by exactly 1 row. The 4 lengths of one device sum to 1024. `kv_pool`: cached keys and values of order one or more.
All inputs are finite; a program needn't handle non-finite values.
Results may differ from a plain program's by a relative error of at most 0.013.
Values may be sent and summed in bfloat16 or wider, within the bound.
A program may use at most 128 MiB of HBM per device.

v0:
```python
import jax
import jax.numpy as jnp
from jax import lax
from jax.sharding import Mesh
from jax.sharding import PartitionSpec as P

HEADS = 64
KV_HEADS = 8
HEAD_DIM = 128
PAGE = 128
MAX_PAGES = 4
GROUP = ("group_0", "group_1")
GROUP_TENSOR = ("group_0", "group_1", "tensor")


EPS = 1e-05
ROPE_BASE = 500000.0
NEG_FILL = -1e30


def cut_along(shard, dim, devices):
    lengths = shard.shape
    parts = shard.reshape(*lengths[:dim], devices, lengths[dim] // devices, *lengths[dim + 1 :])
    return jnp.moveaxis(parts, dim, 0)


def joined_along(parts, dim):
    parts = jnp.moveaxis(parts, 0, dim)
    lengths = parts.shape
    return parts.reshape(*lengths[:dim], lengths[dim] * lengths[dim + 1], *lengths[dim + 2 :])


def moved_by_axis(parts, axes, sequence):
    inside = parts.shape[1:]
    out = parts.reshape(*(lax.axis_size(a) for a in axes), *inside)
    for k in sequence:
        out = lax.all_to_all(out, axes[k], k, k, tiled=True)
    return out.reshape(-1, *inside)


def stepwise_exchange(shard, axes, sequence, split_dim, concat_dim):
    parts = cut_along(shard, split_dim, lax.axis_size(axes))
    return joined_along(moved_by_axis(parts, axes, sequence), concat_dim)


def side_by_side(arrays, axis, split_dim, concat_dim, along):
    columns = [a.reshape(*a.shape[:along], -1) for a in arrays]
    both = jnp.concatenate(columns, axis=along)
    out, at, gathered = (
        lax.all_to_all(both, axis, split_axis=split_dim, concat_axis=concat_dim, tiled=True),
        0,
        [],
    )
    for a, column in zip(arrays, columns):
        piece = out[..., at : at + column.shape[along]]
        gathered.append(piece.reshape(*piece.shape[:along], *a.shape[along:]))
        at += column.shape[along]
    return tuple(gathered)


def summed_on_arrival(shard, axis, dim):
    parts = cut_along(shard, dim, lax.axis_size(axis))
    arrived = lax.all_to_all(parts, axis, split_axis=0, concat_axis=0, tiled=True)
    return arrived.astype(jnp.float32).sum(axis=0)


def rotate(values, positions):
    half_dim = values.shape[-1] // 2
    inverse = ROPE_BASE ** (-(jnp.arange(half_dim, dtype=jnp.float32) * 2.0 / values.shape[-1]))
    angles = positions.astype(jnp.float32)[..., None] * inverse
    cosine = jnp.cos(angles)[..., None, :]
    sine = jnp.sin(angles)[..., None, :]
    lower_half = values[..., :half_dim]
    upper_half = values[..., half_dim:]
    return jnp.concatenate(
        [lower_half * cosine - upper_half * sine, upper_half * cosine + lower_half * sine], axis=-1
    )


def cache_stats(queries, pages, row_lens):
    row_total, steps_here, head_count, head_dim = queries.shape
    page_count = pages.shape[1]
    kv_heads = pages.shape[3]
    page_len = pages.shape[4]
    grouped = queries.reshape(row_total, steps_here, kv_heads, head_count // kv_heads, head_dim)
    scores = jnp.einsum(
        "rskgd,rbktd->rskgbt", grouped, pages[:, :, 0], preferred_element_type=jnp.float32
    ) * head_dim ** (-0.5)
    places = (
        jnp.arange(page_count, dtype=jnp.int32)[:, None] * page_len
        + jnp.arange(page_len, dtype=jnp.int32)[None, :]
    )
    inside = (places[None] < row_lens[:, None, None])[:, None, None, None]
    page_top = jnp.max(jnp.where(inside, scores, NEG_FILL), axis=-1)
    weights = jnp.where(inside, jnp.exp(scores - page_top[..., None]), 0.0).astype(jnp.bfloat16)
    page_total = jnp.sum(weights.astype(jnp.float32), axis=-1)
    page_acc = jnp.einsum(
        "rskgbt,rbktd->rskgbd", weights, pages[:, :, 1], preferred_element_type=jnp.float32
    )
    top_score = jnp.max(page_top, axis=-1)
    page_scale = jnp.exp(page_top - top_score[..., None])
    return (
        top_score,
        jnp.sum(page_scale * page_total, axis=-1),
        jnp.sum(page_scale[..., None] * page_acc, axis=-2),
    )


def finish(queries, cache_parts, all_keys, all_values):
    row_total, steps_here, head_count, head_dim = queries.shape
    kv_heads = all_keys.shape[2]
    grouped = queries.reshape(row_total, steps_here, kv_heads, head_count // kv_heads, head_dim)
    scores = jnp.einsum(
        "rskgd,rukd->rskgu", grouped, all_keys, preferred_element_type=jnp.float32
    ) * head_dim ** (-0.5)
    allowed = jnp.arange(all_keys.shape[1])[None, :] <= jnp.arange(steps_here)[:, None]
    allowed = allowed[None, :, None, None, :]
    new_top = jnp.max(jnp.where(allowed, scores, NEG_FILL), axis=-1)
    weights = jnp.where(allowed, jnp.exp(scores - new_top[..., None]), 0.0).astype(jnp.bfloat16)
    new_total = jnp.sum(weights.astype(jnp.float32), axis=-1)
    new_acc = jnp.einsum(
        "rskgu,rukd->rskgd", weights, all_values, preferred_element_type=jnp.float32
    )
    cache_top, cache_total, cache_acc = cache_parts
    top_score = jnp.maximum(cache_top, new_top)
    cache_scale = jnp.exp(cache_top - top_score)
    new_scale = jnp.exp(new_top - top_score)
    merged = (cache_scale[..., None] * cache_acc + new_scale[..., None] * new_acc) / (
        cache_scale * cache_total + new_scale * new_total
    )[..., None]
    return merged.reshape(row_total, steps_here, head_count * head_dim).astype(jnp.bfloat16)


def per_device(tokens, norm_gain, w_qkv, w_out, lengths, migrate, page_order, kv_pool):
    row_lens = lengths[0]
    destinations = migrate[0]
    pool_order = page_order[0]
    page_pool = kv_pool[0]
    row_total = row_lens.shape[0]
    pool_size = page_pool.shape[0]
    slot_ids = jnp.arange(row_total, dtype=jnp.int32)
    sort_keys = destinations * row_total + slot_ids
    row_ranks = jnp.sum((sort_keys[None, :] < sort_keys[:, None]).astype(jnp.int32), axis=1)
    placing = row_ranks[:, None] == slot_ids[None, :]
    pages_used = (row_lens + PAGE - 1) // PAGE
    offsets = jnp.cumsum(pages_used) - pages_used
    sorted_lens = jnp.sum(jnp.where(placing, row_lens[:, None], 0), axis=0)
    sorted_first = jnp.sum(jnp.where(placing, offsets[:, None], 0), axis=0)
    page_slots = jnp.clip(
        sorted_first[:, None] + jnp.arange(MAX_PAGES, dtype=jnp.int32)[None, :], 0, pool_size - 1
    )
    home_pages = page_pool[pool_order[page_slots]]
    new_lens = stepwise_exchange(sorted_lens, GROUP, (0, 1), 0, 0)
    width_q = HEADS * HEAD_DIM
    width_k = KV_HEADS * HEAD_DIM
    keys_so_far = jnp.zeros((row_total, 0, KV_HEADS, HEAD_DIM), jnp.bfloat16)
    values_so_far = jnp.zeros((row_total, 0, KV_HEADS, HEAD_DIM), jnp.bfloat16)
    steps_here = tokens.shape[1]
    floats = tokens.astype(jnp.float32)
    normed = (
        floats * lax.rsqrt(jnp.mean(floats * floats, axis=-1, keepdims=True) + EPS) * norm_gain
    ).astype(jnp.bfloat16)

    def columns(row_piece, row_start):
        return jnp.einsum(
            "rsd,dc->rsc", row_piece, w_qkv, preferred_element_type=jnp.float32
        ).astype(jnp.bfloat16)

    gathered = columns(lax.all_gather(normed, "tensor", axis=0, tiled=True), jnp.int32(0))
    full_rows = lax.all_to_all(gathered, "tensor", split_axis=0, concat_axis=2, tiled=True)
    positions = new_lens[:, None] + 0 + jnp.arange(steps_here, dtype=jnp.int32)[None, :]
    queries = rotate(
        full_rows[..., :width_q]
        .reshape(row_total, steps_here, HEADS, HEAD_DIM)
        .astype(jnp.float32),
        positions,
    ).astype(jnp.bfloat16)
    keys_here = rotate(
        full_rows[..., width_q : width_q + width_k]
        .reshape(row_total, steps_here, KV_HEADS, HEAD_DIM)
        .astype(jnp.float32),
        positions,
    ).astype(jnp.bfloat16)
    values_here = full_rows[..., width_q + width_k :].reshape(
        row_total, steps_here, KV_HEADS, HEAD_DIM
    )
    all_keys = jnp.concatenate([keys_so_far, keys_here], axis=1)
    all_values = jnp.concatenate([values_so_far, values_here], axis=1)
    home_queries = lax.all_to_all(queries, GROUP, split_axis=0, concat_axis=0, tiled=True)
    home_parts = cache_stats(home_queries, home_pages, sorted_lens)
    attended = finish(
        queries,
        tuple(
            (
                part.astype(jnp.float32)
                for part in side_by_side(
                    (
                        home_parts[0].astype(jnp.bfloat16),
                        home_parts[1].astype(jnp.bfloat16),
                        home_parts[2].astype(jnp.bfloat16),
                    ),
                    GROUP,
                    0,
                    0,
                    4,
                )
            )
        ),
        all_keys,
        all_values,
    )
    spread = lax.all_to_all(attended, "tensor", split_axis=2, concat_axis=0, tiled=True)
    summed = summed_on_arrival(
        jnp.einsum("rsc,cd->rsd", spread, w_out, preferred_element_type=jnp.float32).astype(
            jnp.bfloat16
        ),
        "tensor",
        0,
    )
    output = (floats + summed).astype(jnp.bfloat16)
    return output


def solution(mesh):
    split = Mesh(mesh.devices.reshape(2, 2, mesh.shape["tensor"]), ("group_0", "group_1", "tensor"))
    placed = (
        P(GROUP_TENSOR, None, None),
        P(),
        P(None, "tensor"),
        P("tensor", None),
        P(GROUP_TENSOR, None),
        P(GROUP_TENSOR, None),
        P(GROUP_TENSOR, None),
        P(GROUP_TENSOR, None, None, None, None, None),
    )
    return jax.shard_map(
        per_device,
        mesh=split,
        in_specs=placed,
        out_specs=P(GROUP_TENSOR, None, None),
        check_vma=False,
    )
```

profile of v0, /device:TPU:1, one launch (start us, length us, event | category | flops | bytes accessed | tf_op | source)
XLA Modules:
  0.0 343.2 jit_solution(6098262649707031891)
XLA Ops:
  6.5 1.1 fusion.23
  7.7 1.1 fusion.25
  8.8 0.9 copy.227
  9.7 0.7 and_select_fusion.1
  10.5 0.7 bitcast_add_fusion
  11.2 0.7 add_bitcast_fusion
  12.0 0.7 bitcast_subtract_fusion.1
  12.7 0.7 select_reduce_fusion.2
  13.5 0.6 reshape_reshape.3
  14.1 3.3 all-to-all-start.1
  17.6 0.7 gather_fusion
  18.4 7.7 %gather_fusion.1 = bf16[16,2,8,128,128]{4,3,2,1,0:T(8,128)(2,1)} fusion(bf16[12,2,8,128,128]{4,3,2,1,0:T(8,128)(2,1)} %bitcast.155, s32[1024]{0:T(1024)S(1)} %pad_clamp_fusion), kind=kCustom, calls=%fused_computation.1 | custom fusion | bytes 16777280 | tf_op jit(solution)/shard_map/gather | solution.py:152
  26.3 6.1 %fusion.46 = (bf16[4,4,1,8,128,128]{5,4,3,2,1,0:T(8,128)(2,1)}, bf16[4,4,1,8,128,128]{5,4,3,2,1,0:T(8,128)(2,1)}) fusion(bf16[4,4,2,8,128,128]{5,4,3,2,1,0:T(8,128)(2,1)} %bitcast.152), kind=kLoop, calls=%fused_computation.107 | loop fusion | bytes 16777216 | tf_op jit(solution)/shard_map/slice | solution.py:87
  32.4 4.6 %all_to_all.61 = s32[2,2,1]{0,2,1:T(1,128)S(1)} all-to-all(s32[2,2,1]{0,2,1:T(1,128)S(1)} %copy.233), channel_id=1, replica_groups=mesh['group_0'=2,'group_1'=2,'tensor'=32] {'group_1'}, dimensions={1} | all-to-all | bytes 32 | tf_op jit(solution)/shard_map/all_to_all | solution.py:37
  37.3 80.0 %all-gather.2.cloned.1.call-done = bf16[128,3,8192]{2,1,0:T(4,128)(2,1)} async-done(((bf16[4,3,8192]{2,1,0:T(4,128)(2,1)}), bf16[128,3,8192]{2,1,0:T(4,128)(2,1)}) %all-gather.2.cloned.1.call-update) | async-done | bytes 6291472 | tf_op jit(solution)/shard_map/all_gather | solution.py:169
  117.2 12.4 %fusion.16 = bf16[128,3,320]{0,2,1:T(8,128)(2,1)S(1)} fusion(bf16[8192,320]{0,1:T(8,128)(2,1)} %param.10, bf16[128,3,8192]{2,1,0:T(4,128)(2,1)} %all-gather.2.cloned.1.call-done), kind=kOutput, calls=%fused_computation.27 | convolution fusion | flops 2013388800 | bytes 11780096 | tf_op jit(solution)/shard_map/rsd,dc->rsc/dot_general | solution.py:165
  129.6 1.0 copy.229
  130.6 5.7 %all-to-all-start = ((bf16[128,3,320]{2,1,0:T(4,128)(2,1)}), bf16[128,3,320]{2,1,0:T(4,128)(2,1)S(1)}, u32[]{:S(2)}, u32[]{:S(2)}) async-start(bf16[128,3,320]{2,1,0:T(4,128)(2,1)} %copy.229), calls=%async_computation | async-start | bytes 786432 | tf_op jit(solution)/shard_map/all_to_all | solution.py:170
  136.5 9.5 %all-to-all-done = bf16[128,3,320]{2,1,0:T(4,128)(2,1)S(1)} async-done(((bf16[128,3,320]{2,1,0:T(4,128)(2,1)}), bf16[128,3,320]{2,1,0:T(4,128)(2,1)S(1)}, u32[]{:S(2)}, u32[]{:S(2)}) %all-to-all-start) | async-done | bytes 245792 | tf_op jit(solution)/shard_map/all_to_all | solution.py:170
  146.1 0.4 all_to_all.44
  146.6 0.3 reshape.287
  147.2 0.7 copy.237
  147.9 6.1 %all-to-all-start.3 = ((bf16[4,3,64,128]{3,2,1,0:T(8,128)(2,1)}), bf16[4,3,64,128]{3,2,1,0:T(8,128)(2,1)S(1)}, u32[]{:S(2)}, u32[]{:S(2)}) async-start(bf16[4,3,64,128]{3,2,1,0:T(8,128)(2,1)} %copy.237), calls=%async_computation.3 | async-start | bytes 393216 | tf_op jit(solution)/shard_map/all_to_all | solution.py:189
  154.1 4.4 %all-to-all-done.3 = bf16[4,3,64,128]{3,2,1,0:T(8,128)(2,1)S(1)} async-done(((bf16[4,3,64,128]{3,2,1,0:T(8,128)(2,1)}), bf16[4,3,64,128]{3,2,1,0:T(8,128)(2,1)S(1)}, u32[]{:S(2)}, u32[]{:S(2)}) %all-to-all-start.3) | async-done | bytes 196640 | tf_op jit(solution)/shard_map/all_to_all | solution.py:189
  158.5 3.6 %fusion.10 = (f32[4,3,8,8,4]{3,1,4,2,0:T(4,128)S(1)}, f32[4,8,4,128,3,8]{3,5,4,2,1,0:T(8,128)S(1)}) fusion(pred[4,4,128]{2,1,0:T(4,128)(4,1)S(1)} %broadcast_compare_fusion, bf16[4,4,1,8,128,128]{5,4,3,2,1,0:T(8,128)(2,1)} %get-tuple-element.11, bf16[4,3,64,128]{3,2,1,0:T(8,128)(2,1)S(1)} %all-to-all-done.3), kind=kOutput, calls=%fused_computation.20 | convolution fusion | flops 101839872 | bytes 5978112 | tf_op jit(solution)/shard_map/rskgd,rbktd->rskgbt/dot_general | solution.py:86
  162.1 1.2 convert_reduce_fusion.1
  163.5 0.7 copy.242
  164.1 0.7 copy.243
  164.8 3.5 %fusion.6 = bf16[4,3,8,8,128]{4,3,1,2,0:T(8,128)(2,1)S(1)} fusion(bf16[4,4,1,8,128,128]{5,4,3,2,1,0:T(8,128)(2,1)} %get-tuple-element.12, f32[4,3,8,8,4]{3,1,4,2,0:T(4,128)S(1)} %get-tuple-element.10, f32[4,8,4,128,3,8]{3,5,4,2,1,0:T(8,128)S(1)} %get-tuple-element.29, f32[4,3,8,8,4]{3,1,4,2,0:T(4,128)S(1)} %get-tuple-element.28, ...), kind=kOutput, calls=%fused_computation.13 | convolution fusion | flops 102531072 | bytes 5990400 | tf_op jit(solution)/shard_map/rskgbt,rbktd->rskgbd/dot_general | solution.py:97
  168.3 1.1 pad_maximum_fusion
  169.4 4.3 %all-to-all-start.4 = ((bf16[4,3,8,8,130]{4,3,2,1,0:T(8,128)(2,1)}), bf16[4,3,8,8,130]{4,3,2,1,0:T(8,128)(2,1)S(1)}, u32[]{:S(2)}, u32[]{:S(2)}) async-start(bf16[4,3,8,8,130]{4,3,2,1,0:T(8,128)(2,1)} %pad_maximum_fusion), calls=%async_computation.4 | async-start | bytes 786432 | tf_op jit(solution)/shard_map/all_to_all | solution.py:50
  173.7 0.8 select_reduce_fusion
  174.6 0.2 convert_reduce_fusion.2
  174.8 5.5 %all-to-all-done.4 = bf16[4,3,8,8,130]{4,3,2,1,0:T(8,128)(2,1)S(1)} async-done(((bf16[4,3,8,8,130]{4,3,2,1,0:T(8,128)(2,1)}), bf16[4,3,8,8,130]{4,3,2,1,0:T(8,128)(2,1)S(1)}, u32[]{:S(2)}, u32[]{:S(2)}) %all-to-all-start.4) | async-done | bytes 199712 | tf_op jit(solution)/shard_map/all_to_all | solution.py:50
  180.4 0.6 copy.291
  181.0 0.6 copy.295
  181.8 0.6 fusion.21
  182.4 6.5 %copy.286 = bf16[4,3,8,8,128]{0,1,4,3,2:T(4,128)(2,1)} copy(bf16[4,3,8,8,128]{4,3,1,2,0:T(8,128)(2,1)S(1)} %fusion.21) | data formatting | bytes 393216 | tf_op jit(solution)/shard_map/convert_element_type | solution.py:131
  188.9 12.6 %reshape.315 = bf16[32,2,1536]{2,1,0:T(2,128)(2,1)S(1)} reshape(bf16[8192,3,4]{2,1,0:T(4,128)(2,1)} %bitcast.153) | data formatting | bytes 393216
  201.5 12.7 %all_to_all.62 = bf16[32,2,1536]{2,1,0:T(2,128)(2,1)S(1)} all-to-all(bf16[32,2,1536]{2,1,0:T(2,128)(2,1)S(1)} %reshape.315), channel_id=1, replica_groups=mesh['group_0'=2,'group_1'=2,'tensor'=32] {'tensor'}, dimensions={0} | all-to-all | bytes 393216 | tf_op jit(solution)/shard_map/all_to_all | solution.py:212
  214.2 10.4 %reshape.316 = bf16[8192,3,4]{2,1,0:T(4,128)(2,1)} reshape(bf16[32,2,1536]{2,1,0:T(2,128)(2,1)S(1)} %all_to_all.62) | data formatting | bytes 393216
  224.6 7.9 %copy.287 = bf16[4,3,32,256]{3,2,0,1:T(8,128)(2,1)S(1)} copy(bf16[4,3,32,256]{0,1,3,2:T(4,128)(2,1)} %bitcast.154) | data formatting | bytes 393216 | tf_op jit(solution)/shard_map/all_to_all | solution.py:212
  232.7 6.7 %convolution_convert_fusion = bf16[128,3,8192]{2,0,1:T(8,128)(2,1)} fusion(bf16[128,3,256]{2,0,1:T(8,128)(2,1)S(1)} %all_to_all.52, bf16[256,8192]{1,0:T(8,128)(2,1)} %param.11), kind=kOutput, calls=%fused_computation.3 | convolution fusion | flops 1613758464 | bytes 10682368 | tf_op jit(solution)/shard_map/rsc,cd->rsd/dot_general | solution.py:214
  239.4 10.2 %reshape.286 = bf16[32,4,3,8192]{3,1,0,2:T(4,128)(2,1)} reshape(bf16[128,3,8192]{2,0,1:T(8,128)(2,1)} %convolution_convert_fusion) | data formatting | bytes 12582912 | tf_op jit(solution)/shard_map/reshape | solution.py:23
  249.6 5.7 %copy.267 = bf16[32,4,3,8192]{3,1,2,0:T(4,128)(2,1)S(1)} copy(bf16[32,4,3,8192]{3,1,0,2:T(4,128)(2,1)} %reshape.286) | data formatting | bytes 12582912 | tf_op jit(solution)/shard_map/reshape | solution.py:23
  255.2 77.3 %all_to_all.63 = bf16[32,4,3,8192]{3,1,2,0:T(4,128)(2,1)S(1)} all-to-all(bf16[32,4,3,8192]{3,1,2,0:T(4,128)(2,1)S(1)} %copy.267), channel_id=1, replica_groups=mesh['group_0'=2,'group_1'=2,'tensor'=32] {'tensor'}, dimensions={0} | all-to-all | bytes 12582912 | tf_op jit(solution)/shard_map/all_to_all | solution.py:63
  332.6 3.0 convert_reduce_fusion
  335.6 0.8 fusion.26
  (50 shorter events, 2.6 us)
Async XLA Ops:
  6.5 11.0 %copy-start = (s32[1,12]{1,0:T(1,128)S(1)}, s32[1,12]{1,0:T(1,128)}, u32[]{:S(2)}) copy-start(s32[1,12]{1,0:T(1,128)} %param.14) | copy-start | bytes 148
  6.5 110.7 %all-gather.2.cloned.1.call-start = ((), (), s32[]{:S(2)}) async-start(), calls=%async_computation.7 | async-start | bytes 8650752 | tf_op jit(solution)/shard_map/all_gather | solution.py:169
  14.1 18.2 %all-to-all-start.1 = ((s32[2,2,1]{1,2,0:T(1,128)}), s32[2,2,1]{1,2,0:T(1,128)S(1)}, u32[]{:S(2)}, u32[]{:S(2)}) async-start(s32[2,2,1]{1,2,0:T(1,128)} %bitcast.15), calls=%async_computation.1 | async-start | bytes 2048 | tf_op jit(solution)/shard_map/all_to_all | solution.py:37
  130.6 15.5 %all-to-all-start = ((bf16[128,3,320]{2,1,0:T(4,128)(2,1)}), bf16[128,3,320]{2,1,0:T(4,128)(2,1)S(1)}, u32[]{:S(2)}, u32[]{:S(2)}) async-start(bf16[128,3,320]{2,1,0:T(4,128)(2,1)} %copy.229), calls=%async_computation | async-start | bytes 786432 | tf_op jit(solution)/shard_map/all_to_all | solution.py:170
  147.9 10.6 %all-to-all-start.3 = ((bf16[4,3,64,128]{3,2,1,0:T(8,128)(2,1)}), bf16[4,3,64,128]{3,2,1,0:T(8,128)(2,1)S(1)}, u32[]{:S(2)}, u32[]{:S(2)}) async-start(bf16[4,3,64,128]{3,2,1,0:T(8,128)(2,1)} %copy.237), calls=%async_computation.3 | async-start | bytes 393216 | tf_op jit(solution)/shard_map/all_to_all | solution.py:189
  169.4 10.9 %all-to-all-start.4 = ((bf16[4,3,8,8,130]{4,3,2,1,0:T(8,128)(2,1)}), bf16[4,3,8,8,130]{4,3,2,1,0:T(8,128)(2,1)S(1)}, u32[]{:S(2)}, u32[]{:S(2)}) async-start(bf16[4,3,8,8,130]{4,3,2,1,0:T(8,128)(2,1)} %pad_maximum_fusion), calls=%async_computation.4 | async-start | bytes 786432 | tf_op jit(solution)/shard_map/all_to_all | solution.py:50
  255.2 81.2 %copy-start.1 = (s32[1,12]{1,0:T(1,128)S(1)}, s32[1,12]{1,0:T(1,128)}, u32[]{:S(2)}) copy-start(s32[1,12]{1,0:T(1,128)} %param.14) | copy-start | bytes 148
  332.5 3.0 copy-start.2
Sparse Core Ops, SparseCore 0:
  10.5 106.6 all-gather.1
where the time goes:
time: 346 us; the launch traced here: 343 us
  waiting for transfers between devices  99.4 us (29%)
  blocking collectives  94.7 us (27%)
  local copies, waits for them, and re-layouts  75.1 us (22%)
  matrix products  27.6 us (8%)
  starting transfers between devices  19.4 us (6%)
  between operations  13.6 us (4%)
  other arithmetic  13.4 us (4%)
    all_gather x1, waiting for transfers between devices, per_device(): lax.all_gather(normed, 'tensor', axis=0, tiled=True)  80 us
    all_to_all x1, blocking collectives, summed_on_arrival(): lax.all_to_all(parts, axis, split_axis=0, concat_axis=0, tiled=True)  77.3 us
    unnamed x10, local copies, waits for them, and re-layouts  24.2 us
    reshape x2, local copies, waits for them, and re-layouts, cut_along(): shard.reshape(*lengths[:dim], devices, lengths[dim] // devices, *lengths[...  15.8 us
    all_to_all x1, blocking collectives, per_device(): lax.all_to_all(attended, 'tensor', split_axis=2, concat_axis=0, tiled=True)  12.7 us
    dot_general x1, matrix products, columns(): jnp.einsum('rsd,dc->rsc', row_piece, w_qkv, preferred_element_type=jnp.fl...  12.4 us
    all_to_all x1, waiting for transfers between devices, per_device(): lax.all_to_all(gathered, 'tensor', split_axis=0, concat_axis=2, tiled=True)  9.54 us
    gather x3, local copies, waits for them, and re-layouts, per_device(): home_pages = page_pool[pool_order[page_slots]]  8.42 us
  transfers between devices with their start and end apart: 5, of which 4 were waited for; matrix products, arithmetic and copies ran while one was open for 6% of the time, Pallas kernels for 0%

commit v1 on v0

v1 whole, which is shorter than its diff:
```python
import jax
import jax.numpy as jnp
import numpy as np
from jax import lax
from jax.experimental import pallas as pl
from jax.experimental.pallas import tpu as pltpu
from jax.sharding import PartitionSpec as P

MESH = pl.DeviceIdType.MESH
F32 = jnp.float32
BF16 = jnp.bfloat16
EPS = 1e-05
ROPE_BASE = 500000.0
NEG_FILL = -1e30
SCALE = 128 ** (-0.5)
D = 8192
MAIN = 6144
QW = 1536
CHUNK = 512
N_T = 32
N_G = 4


def body(
    tok, gain, inv, lens, mig, order, wqkv_hbm, wout_hbm, kv_hbm, out,
    stage, gsend, grecv, x32, xg, wq, wo, kv, qacc, qout, qin, heads, att, ain,
    terms, rq, rf, rx, fsend, frecv, o32,
    load_sem, gs_sem, gr_sem, s_sem, r_sem, as_sem, ar_sem,
):
    g = lax.axis_index("group")
    t = lax.axis_index("tensor")
    xh, y, z = t // 16, (t // 4) % 4, t % 4

    def idx(xx, yy, zz):
        return xx * 16 + lax.rem(yy + 4, 4) * 4 + lax.rem(zz + 4, 4)

    barrier = pltpu.get_barrier_semaphore()

    def greet(i, c):
        pl.semaphore_signal(
            barrier, inc=1, device_id=(g, lax.rem(t + i, N_T)), device_id_type=MESH
        )
        return c

    lax.fori_loop(1, N_T, greet, 0)
    for i in range(1, N_G):
        pl.semaphore_signal(
            barrier, inc=1, device_id=(lax.rem(g + i, N_G), t), device_id_type=MESH
        )

    loads = [
        pltpu.make_async_copy(wqkv_hbm, wq, load_sem.at[0]),
        pltpu.make_async_copy(kv_hbm, kv, load_sem.at[1]),
        pltpu.make_async_copy(wout_hbm, wo, load_sem.at[2]),
    ]
    for c in loads:
        c.start()

    for s in range(N_G):
        rows = tok[s].astype(F32)
        mean = jnp.mean(rows * rows, axis=-1, keepdims=True)
        normed = rows * lax.rsqrt(mean + EPS) * gain[...]
        for q in range(4):
            stage[s, 4 * q : 4 * q + 3, :] = normed[:, q * QW : (q + 1) * QW]
        for c in range(12):
            at = MAIN + (c % 4) * CHUNK
            lane = (c % 3) * CHUNK
            row = 4 * (c // 3) + 3
            stage[s, row : row + 1, lane : lane + CHUNK] = normed[
                c // 4 : c // 4 + 1, at : at + CHUNK
            ]
        gsend[s] = stage[s].astype(BF16)

    pl.semaphore_wait(barrier, N_T - 1 + N_G - 1)

    def group_exchange(src, dst, base):
        copies = []
        for i in range(1, N_G):
            to = lax.rem(g + i, N_G)
            copies.append(
                pltpu.make_async_remote_copy(
                    src_ref=src.at[to], dst_ref=dst.at[g],
                    send_sem=gs_sem.at[base + i], recv_sem=gr_sem.at[base + i],
                    device_id=(to, t), device_id_type=MESH,
                )
            )
            copies[-1].start()
        dst[g] = src[g]
        for c in copies:
            c.wait_recv()
        return copies

    sent = group_exchange(gsend, grecv, 0)
    for gg in range(N_G):
        stage[gg] = grecv[gg].astype(F32)
    for gg in range(N_G):
        for q in range(4):
            x32[q, 4 * gg : 4 * gg + 4, :] = stage[gg, 4 * q : 4 * q + 4, :]
    for q in range(4):
        xg[q, t] = x32[q].astype(BF16)

    def send(src, dst, k, to):
        c = pltpu.make_async_remote_copy(
            src_ref=src, dst_ref=dst, send_sem=s_sem.at[k], recv_sem=r_sem.at[k],
            device_id=(g, to), device_id_type=MESH,
        )
        c.start()
        sent.append(c)
        return c

    class Gather:
        def __init__(self, at, q, k):
            self.at, self.q, self.k, self.to = at[0], q, k, at[1]

        def start(self):
            ref = xg.at[pl.ds(self.q, 2), self.at(0)]
            self.up = send(ref, ref, self.k, self.to(1))
            self.down = send(ref, ref, self.k + 1, self.to(-1))

        def mid_up(self):
            self.up.wait_recv()
            ref = xg.at[self.q, self.at(-1)]
            self.up2 = send(ref, ref, self.k + 2, self.to(1))

        def mid_down(self):
            self.down.wait_recv()
            ref = xg.at[self.q + 1, self.at(1)]
            self.down2 = send(ref, ref, self.k + 3, self.to(-1))

        def mid(self):
            self.mid_up()
            self.mid_down()

        def end(self):
            self.up2.wait_recv()
            self.down2.wait_recv()

    def place(half, xx, first, second):
        return idx(xx, y + first, z + second) if half == 0 else idx(xx, y + second, z + first)

    def ring_first(half, xx):
        return (lambda o: place(half, xx, o, 0)), (lambda o: place(half, xh, o, 0))

    def ring_second(half, xx, e):
        return (lambda o: place(half, xx, e, o)), (lambda o: place(half, xh, 0, o))

    OFFS = (0, -1, 1, 2)
    own, peer = xh, 1 - xh

    class GatherSet:
        def __init__(self, xx, n):
            self.one = [Gather(ring_first(h, xx), 2 * h, 40 * n + 20 * h) for h in (0, 1)]
            self.two = [
                {
                    e: Gather(ring_second(h, xx, e), 2 * h, 40 * n + 20 * h + 4 + 4 * i)
                    for i, e in enumerate(OFFS)
                }
                for h in (0, 1)
            ]

        def s1(self):
            for h in (0, 1):
                self.one[h].start()
            for h in (0, 1):
                self.two[h][0].start()

        def s2(self):
            for h in (0, 1):
                self.one[h].mid_up()
                self.two[h][-1].start()
                self.one[h].mid_down()
                self.two[h][1].start()

        def mid(self, e):
            for h in (0, 1):
                self.two[h][e].mid()

        def s4(self):
            for h in (0, 1):
                self.one[h].end()
                self.two[h][2].start()

        def end(self, e):
            for h in (0, 1):
                self.two[h][e].end()

    far = idx(peer, y, z)
    row16 = lax.broadcasted_iota(jnp.int32, (256, 1), 0) & 3

    def project(xx):
        def lhs(q, a=0, b=QW):
            return xg[q, pl.ds(xx * 16, 16), :, a:b].reshape(256, b - a)

        def dot(l, a, b):
            return jnp.dot(l, wq[a:b, :], preferred_element_type=F32)

        m = MAIN
        main = dot(lhs(0), 0, QW)
        for q in (1, 2, 3):
            main = main + dot(lhs(q), q * QW, (q + 1) * QW)
        tails = (
            dot(lhs(0), m, m + 1536) + dot(lhs(1, 0, 512), m + 1536, m + 2048),
            dot(lhs(1, 512, 1536), m, m + 1024) + dot(lhs(2, 0, 1024), m + 1024, m + 2048),
            dot(lhs(2, 1024, 1536), m, m + 512) + dot(lhs(3), m + 512, m + 2048),
        )
        add = jnp.zeros_like(main)
        for s in range(3):
            qacc[:, 0:320] = tails[s]
            add = jnp.where(row16 == s, pltpu.roll(qacc[...], 256 - (3 - s), 0)[:, 0:320], add)
        qacc[:, 0:320] = jnp.where(row16 == 3, 0.0, main + add)
        qacc[:, 320:384] = jnp.zeros((256, 64), F32)
        flat = qacc[...]
        flat = jnp.where(lax.rem(t, 2) == 1, pltpu.roll(flat, 64, 1), flat)
        qout[pl.ds(xx * 16, 16)] = flat.reshape(16, 16, 384).astype(BF16)

    def a2a(src, dst, base, to):
        return pltpu.make_async_remote_copy(
            src_ref=src, dst_ref=dst.at[t],
            send_sem=as_sem.at[base + to], recv_sem=ar_sem.at[base + t],
            device_id=(g, to), device_id_type=MESH,
        )

    def a2a_wait(src, dst, base):
        def one(i, c):
            fr = lax.rem(t + i, N_T)
            d = pltpu.make_async_remote_copy(
                src_ref=src.at[fr], dst_ref=dst.at[fr],
                send_sem=as_sem.at[base + fr], recv_sem=ar_sem.at[base + fr],
                device_id=(g, fr), device_id_type=MESH,
            )
            d.wait_recv()
            d.wait_send()
            return c

        lax.fori_loop(1, N_T, one, 0)

    near_set, far_set = GatherSet(own, 0), GatherSet(peer, 1)
    near_set.s1()
    whole = xg.at[:, t]
    across = send(whole, whole, 160, far)
    near_set.s2()
    near_set.mid(0)
    near_set.s4()
    across.wait_recv()
    far_set.s1()
    near_set.mid(-1)
    near_set.mid(1)
    far_set.s2()
    near_set.mid(2)
    for e in OFFS:
        near_set.end(e)
    far_set.mid(0)
    far_set.s4()
    far_set.mid(-1)
    far_set.mid(1)
    loads[0].wait()
    project(own)

    def send_near(i, c):
        to = own * 16 + lax.rem(t + i, 16)
        a2a(qout.at[to], qin, 0, to).start()
        return c

    lax.fori_loop(1, 16, send_near, 0)
    qin[t] = qout[t]
    far_set.mid(2)
    for e in OFFS:
        far_set.end(e)
    project(peer)

    def send_far(i, c):
        to = peer * 16 + lax.rem(t + i, 16)
        a2a(qout.at[to], qin, 0, to).start()
        return c

    lax.fori_loop(0, 16, send_far, 0)

    used = [(lens[0, j] + 127) // 128 for j in range(4)]
    first = [0, used[0], used[0] + used[1], used[0] + used[1] + used[2]]

    def of_group(values, gg):
        total = jnp.int32(0)
        for j in range(4):
            total = total + jnp.where(mig[0, j] == gg, values[j], 0)
        return total

    row_len = [of_group([lens[0, j] for j in range(4)], gg) for gg in range(N_G)]
    pages = [
        [order[0, jnp.clip(of_group(first, gg) + b, 0, 11)] for b in range(4)]
        for gg in range(N_G)
    ]

    def by_row(rows, values):
        kind = (rows & 15) >> 2
        got = jnp.where(kind == 0, values[0], values[1])
        got = jnp.where(kind == 2, values[2], got)
        return jnp.where(kind == 3, values[3], got)

    r16 = lax.broadcasted_iota(jnp.int32, (16, 128), 0)
    angle = (by_row(r16, row_len) + (r16 & 3)).astype(F32) * inv[...]
    lane16 = lax.broadcasted_iota(jnp.int32, (16, 128), 1)
    cosine = jnp.cos(angle)
    sine = jnp.where(lane16 < 64, -jnp.sin(angle), jnp.sin(angle))

    a2a_wait(qout, qin, 0)

    def pair(p, c):
        even, odd = qin[2 * p].astype(F32), qin[2 * p + 1].astype(F32)
        five = (
            even[:, 0:128], even[:, 128:256],
            jnp.where(lane16 < 64, even[:, 256:384], odd[:, 0:128]),
            odd[:, 128:256], odd[:, 256:384],
        )
        for i, h in enumerate(five):
            turned = h * cosine + pltpu.roll(h, 64, 1) * sine
            heads[5 * p + i] = jnp.where(5 * p + i < 72, turned, h).astype(BF16)
        return c

    lax.fori_loop(0, 16, pair, 0)

    loads[1].wait()
    r128 = lax.broadcasted_iota(jnp.int32, (128, 128), 0)
    c128 = lax.broadcasted_iota(jnp.int32, (128, 128), 1)
    lim = by_row(r128, row_len)
    fresh = (
        (c128 < 16) & ((c128 >> 2) == ((r128 & 15) >> 2)) & ((c128 & 3) <= (r128 & 3))
    )
    pad = jnp.zeros((112, 128), BF16)

    def attend(k, c):
        queries = heads[pl.ds(8 * k, 8)].reshape(128, 128)

        def scores(keys):
            return lax.dot_general(
                queries, keys, (((1,), (1,)), ((), ())), preferred_element_type=F32
            )

        blocks, masks = [], []
        for b in range(4):
            blocks.append(
                by_row(r128, [scores(kv[pages[gg][b], 0, k]) for gg in range(N_G)]) * SCALE
            )
            masks.append(c128 + b * 128 < lim)
        blocks.append(scores(jnp.concatenate([heads[64 + k], pad], axis=0)) * SCALE)
        masks.append(fresh)
        tops = [jnp.where(m, s, NEG_FILL) for m, s in zip(masks, blocks)]
        top = tops[0]
        for s in tops[1:]:
            top = jnp.maximum(top, s)
        top = jnp.max(top, axis=-1, keepdims=True)
        weights = [
            jnp.where(m, jnp.exp(s - top), 0.0).astype(BF16) for m, s in zip(masks, tops)
        ]
        total = weights[0].astype(F32)
        for w in weights[1:]:
            total = total + w.astype(F32)
        total = jnp.sum(total, axis=-1, keepdims=True)
        acc = []
        for gg in range(N_G):
            a = jnp.dot(weights[0], kv[pages[gg][0], 1, k], preferred_element_type=F32)
            for b in (1, 2, 3):
                a = a + jnp.dot(
                    weights[b], kv[pages[gg][b], 1, k], preferred_element_type=F32
                )
            acc.append(a)
        acc = by_row(r128, acc) + jnp.dot(
            weights[4],
            jnp.concatenate([heads[72 + k], pad], axis=0),
            preferred_element_type=F32,
        )
        att[pl.ds(4 * k, 4)] = (acc / total).reshape(4, 2, 16, 128).astype(BF16)

        def give(i, c):
            to = 4 * k + i

            @pl.when(to != t)
            def _():
                a2a(att.at[to], ain, N_T, to).start()

            return c

        lax.fori_loop(0, 4, give, 0)
        return c

    lax.fori_loop(0, 8, attend, 0)
    ain[t] = att[t]
    loads[2].wait()
    a2a_wait(att, ain, N_T)

    def lhs_of(xx):
        left = jnp.concatenate(
            [ain[pl.ds(xx * 16, 16), i].reshape(256, 128) for i in (0, 1)], axis=1
        )
        wide = left.astype(F32)
        return left, [pltpu.roll(wide, 3 - s, 0).astype(BF16) for s in range(3)]

    def expand(sides, xx, half):
        left, turned = sides
        for c in range(6 * half, 6 * half + 6):
            at = MAIN + (c % 4) * CHUNK
            main = jnp.dot(
                left, wo[:, c * CHUNK : (c + 1) * CHUNK], preferred_element_type=F32
            )
            tail = jnp.dot(turned[c // 4], wo[:, at : at + CHUNK], preferred_element_type=F32)
            lane = (c % 3) * CHUNK
            terms[c // 3, pl.ds(xx * 16, 16), :, lane : lane + CHUNK] = (
                jnp.where(row16 == 3, tail, main).reshape(16, 16, CHUNK).astype(BF16)
            )

    class Reduce:
        def __init__(self, at, q, k, n):
            self.at, self.to = at
            self.q, self.k, self.n = q, k, n

        def s1(self):
            q, k, n = self.q, self.k, self.n
            self.up = send(terms.at[q, self.at(2)], rq.at[n, 0], k, self.to(1))
            self.down = send(terms.at[q + 1, self.at(-2)], rq.at[n, 1], k + 1, self.to(-1))

        def s2(self):
            q, k, n = self.q, self.k, self.n
            self.up.wait_recv()
            a = self.at(1)
            terms[q, a] = (terms[q, a].astype(F32) + rq[n, 0].astype(F32)).astype(BF16)
            self.up2 = send(terms.at[pl.ds(q, 2), a], rf.at[n, 0], k + 2, self.to(1))
            self.down.wait_recv()
            b = self.at(-1)
            terms[q + 1, b] = (terms[q + 1, b].astype(F32) + rq[n, 1].astype(F32)).astype(BF16)
            self.down2 = send(terms.at[pl.ds(q, 2), b], rf.at[n, 1], k + 3, self.to(-1))

        def s3(self):
            q, n = self.q, self.n
            self.up2.wait_recv()
            self.down2.wait_recv()
            a = self.at(0)
            for i in (0, 1):
                terms[q + i, a] = (
                    terms[q + i, a].astype(F32)
                    + rf[n, 0, i].astype(F32)
                    + rf[n, 1, i].astype(F32)
                ).astype(BF16)

    class ReduceSet:
        def __init__(self, xx, n):
            k, m = 161 + 40 * n, 10 * n
            self.big = [
                {
                    e: Reduce(
                        ring_second(h, xx, e), 2 * h, k + 20 * h + 4 * i, m + 5 * h + i
                    )
                    for i, e in enumerate(OFFS)
                }
                for h in (0, 1)
            ]
            self.last = [
                Reduce(ring_first(h, xx), 2 * h, k + 20 * h + 16, m + 5 * h + 4) for h in (0, 1)
            ]

        def s1(self, h):
            for e in (2, -1, 1, 0):
                self.big[h][e].s1()

        def s2(self, *es):
            for e in es:
                for h in (0, 1):
                    self.big[h][e].s2()

        def s3(self, *es):
            for e in es:
                for h in (0, 1):
                    self.big[h][e].s3()

        def l1(self):
            for h in (0, 1):
                self.last[h].s1()

        def l2(self):
            for h in (0, 1):
                self.last[h].s2()

        def l3(self):
            for h in (0, 1):
                self.last[h].s3()

    far_sum, near_sum = ReduceSet(peer, 0), ReduceSet(own, 1)
    sides = lhs_of(peer)
    expand(sides, peer, 0)
    far_sum.s1(0)
    expand(sides, peer, 1)
    far_sum.s1(1)
    far_sum.s2(2, -1, 1, 0)
    sides = lhs_of(own)
    expand(sides, own, 0)
    near_sum.s1(0)
    expand(sides, own, 1)
    near_sum.s1(1)
    far_sum.s3(2)
    far_sum.l1()
    near_sum.s2(2)
    far_sum.s3(-1, 1)
    far_sum.l2()
    near_sum.s2(-1, 1)
    far_sum.s3(0)
    far_sum.l3()
    over = send(terms.at[:, far], rx, 241, far)
    near_sum.s2(0)
    near_sum.s3(2)
    near_sum.l1()
    near_sum.s3(-1, 1)
    near_sum.l2()
    near_sum.s3(0)
    near_sum.l3()
    over.wait_recv()
    for q in range(4):
        x32[q] = terms[q, t].astype(F32) + rx[q].astype(F32)
    for gg in range(N_G):
        for q in range(4):
            stage[gg, 4 * q : 4 * q + 4, :] = x32[q, 4 * gg : 4 * gg + 4, :]
    for gg in range(N_G):
        fsend[gg] = stage[gg].astype(BF16)
    sent.extend(group_exchange(fsend, frecv, N_G))
    for s in range(N_G):
        stage[s] = frecv[s].astype(F32)
        for q in range(4):
            o32[s, :, q * QW : (q + 1) * QW] = stage[s, 4 * q : 4 * q + 3, :]
        for c in range(12):
            at = MAIN + (c % 4) * CHUNK
            lane = (c % 3) * CHUNK
            row = 4 * (c // 3) + 3
            o32[s, c // 4 : c // 4 + 1, at : at + CHUNK] = stage[
                s, row : row + 1, lane : lane + CHUNK
            ]
        out[s] = (tok[s].astype(F32) + o32[s]).astype(BF16)
    for c in sent:
        c.wait_send()


def per_device(tokens, norm_gain, w_qkv, w_out, lengths, migrate, page_order, kv_pool):
    half = np.arange(64, dtype=np.float32)
    inverse = jnp.float32(ROPE_BASE) ** (-(jnp.asarray(half) * 2.0 / 128))
    inverse = jnp.concatenate([inverse, inverse]).reshape(1, 128)
    vmem = pl.BlockSpec(memory_space=pltpu.VMEM)
    smem = pl.BlockSpec(memory_space=pltpu.SMEM)
    hbm = pl.BlockSpec(memory_space=pl.ANY)
    dma = pltpu.SemaphoreType.DMA
    return pl.pallas_call(
        body,
        out_shape=jax.ShapeDtypeStruct((4, 3, D), BF16),
        in_specs=[vmem, vmem, vmem, smem, smem, smem, hbm, hbm, hbm],
        out_specs=vmem,
        scratch_shapes=[
            pltpu.VMEM((4, 16, QW), F32),
            pltpu.VMEM((4, 16, QW), BF16),
            pltpu.VMEM((4, 16, QW), BF16),
            pltpu.VMEM((4, 16, QW), F32),
            pltpu.VMEM((4, 32, 16, QW), BF16),
            pltpu.VMEM((D, 320), BF16),
            pltpu.VMEM((256, D), BF16),
            pltpu.VMEM((12, 2, 8, 128, 128), BF16),
            pltpu.VMEM((256, 384), F32),
            pltpu.VMEM((32, 16, 384), BF16),
            pltpu.VMEM((32, 16, 384), BF16),
            pltpu.VMEM((80, 16, 128), BF16),
            pltpu.VMEM((32, 2, 16, 128), BF16),
            pltpu.VMEM((32, 2, 16, 128), BF16),
            pltpu.VMEM((4, 32, 16, QW), BF16),
            pltpu.VMEM((20, 2, 16, QW), BF16),
            pltpu.VMEM((20, 2, 2, 16, QW), BF16),
            pltpu.VMEM((4, 16, QW), BF16),
            pltpu.VMEM((4, 16, QW), BF16),
            pltpu.VMEM((4, 16, QW), BF16),
            pltpu.VMEM((4, 3, D), F32),
            dma((3,)),
            dma((2 * N_G,)),
            dma((2 * N_G,)),
            dma((242,)),
            dma((242,)),
            dma((2 * N_T,)),
            dma((2 * N_T,)),
        ],
        compiler_params=pltpu.CompilerParams(
            collective_id=0, has_side_effects=True, vmem_limit_bytes=60 * 2**20
        ),
        cost_estimate=pl.CostEstimate(
            flops=4 * 10**9, bytes_accessed=17 * 10**6, transcendentals=10**6
        ),
    )(
        tokens, norm_gain.reshape(1, D), inverse, lengths, migrate, page_order,
        w_qkv, w_out, kv_pool.reshape(12, 2, 8, 128, 128),
    )


def solution(mesh):
    both = ("group", "tensor")
    return jax.shard_map(
        per_device,
        mesh=mesh,
        in_specs=(
            P(both, None, None),
            P(),
            P(None, "tensor"),
            P("tensor", None),
            P(both, None),
            P(both, None),
            P(both, None),
            P(both, None, None, None, None, None),
        ),
        out_specs=P(both, None, None),
        check_vma=False,
    )
```

time: 346 us -> 138 us (0.40)
  Pallas kernels: 0 us -> 124 us
  waiting for transfers between devices: 99.4 us -> 0 us
  blocking collectives: 94.7 us -> 0 us
  local copies, waits for them, and re-layouts: 75.1 us -> 11.8 us
  matrix products: 27.6 us -> 0 us
  starting transfers between devices: 19.4 us -> 0 us
  between operations: 13.6 us -> 0.01 us
  other arithmetic: 13.4 us -> 0.6 us
    pallas_call x0 -> x1, Pallas kernels: none -> 124 us  [per_device(): pl.pallas_call(body, out_shape=jax.ShapeDtypeStruct((4, 3, D), BF16), in_...]
    all_to_all x3 -> x0, blocking collectives: 94.7 us -> none  [the longest x1 77.3 us: summed_on_arrival(): lax.all_to_all(parts, axis, split_axis=0, concat_axis=0, tiled=True)]
    all_gather x1 -> x0, waiting for transfers between devices: 80 us -> none  [per_device(): lax.all_gather(normed, 'tensor', axis=0, tiled=True)]
    dot_general x6 -> x0, matrix products: 27.6 us -> none  [the longest x1 12.4 us: columns(): jnp.einsum('rsd,dc->rsc', row_piece, w_qkv, preferred_element_type=jnp.fl...]
    all_to_all x4 -> x0, waiting for transfers between devices: 19.4 us -> none  [the longest x1 9.54 us: per_device(): lax.all_to_all(gathered, 'tensor', split_axis=0, concat_axis=2, tiled=True)]
    all_to_all x4 -> x0, starting transfers between devices: 19.4 us -> none  [the longest x1 6.11 us: per_device(): lax.all_to_all(queries, GROUP, split_axis=0, concat_axis=0, tiled=True)]
    reshape x3 -> x0, local copies, waits for them, and re-layouts: 15.8 us -> none  [the longest x2 15.8 us: cut_along(): shard.reshape(*lengths[:dim], devices, lengths[dim] // devices, *lengths[...]
    unnamed x10 -> x2, local copies, waits for them, and re-layouts: 24.2 us -> 9.99 us
  transfers between devices with their start and end apart: 5 -> 0, of which waited for: 4 -> 0; matrix products, arithmetic and copies ran while one was open for 6% -> 0% of each run, Pallas kernels for 0% -> 0%
where the time goes in v1:
time: 138 us; the launch traced here: 136 us
  Pallas kernels  124 us (90%)
  local copies, waits for them, and re-layouts  11.8 us (9%)
    pallas_call x1, Pallas kernels, per_device(): pl.pallas_call(body, out_shape=jax.ShapeDtypeStruct((4, 3, D), BF16), in_...  124 us
    unnamed x2, local copies, waits for them, and re-layouts  9.99 us

profile of v1, /device:TPU:1, one launch (start us, length us, event | category | flops | bytes accessed | tf_op | source)
XLA Modules:
  0.0 136.4 jit_solution(15783016629205241546)
XLA Ops:
  0.0 0.6 maximum_bitcast_fusion.inv
  0.6 1.8 %copy.10.tok = bf16[4,3,8192]{2,1,0:T(4,128)(2,1)} copy(bf16[4,3,8192]{2,0,1:T(4,128)(2,1)} %param.9) | data formatting | bytes 393216 | tf_op args[0]
  2.4 8.2 %copy.11.wqkv_hbm = bf16[8192,320]{1,0:T(8,128)(2,1)} copy(bf16[8192,320]{0,1:T(8,128)(2,1)} %param.11) | data formatting | bytes 10485760 | tf_op args[2]
  10.6 124.0 %shard_map.91 = bf16[4,3,8192]{2,1,0:T(4,128)(2,1)} custom-call(bf16[4,3,8192]{2,1,0:T(4,128)(2,1)} %copy.10.tok, f32[1,8192]{1,0:T(1,128)} %bitcast.5, f32[1,128]{1,0:T(1,128)} %maximum_bitcast_fusion.inv, s32[1,4]{1,0:T(1,128)} %lens.1, s32[1,4]{1,0:T(1,128)} %mig.1, s32[1,12]{1,0:T(1,128)} %order.1, bf16[8192,320]{1,0:T(8,128)(2,1)} %copy.11.wqkv_hbm, ...), custom_call_target="tpu_custom_call" | custom-call | flops 4000000000 | bytes 17000000 | tf_op jit(solution)/shard_map/pallas_call | solution.py:546
  134.6 1.8 %copy.12 = bf16[4,3,8192]{2,0,1:T(4,128)(2,1)} copy(bf16[4,3,8192]{2,1,0:T(4,128)(2,1)} %shard_map.91) | data formatting | bytes 393216 | tf_op jit(solution)/shard_map/pallas_call | solution.py:546
  (1 shorter events, 0.0 us)

commit v2 on v1

--- a/solution.py
+++ b/solution.py
@@ -36,17 +36,12 @@
 
     barrier = pltpu.get_barrier_semaphore()
 
-    def greet(i, c):
-        pl.semaphore_signal(
-            barrier, inc=1, device_id=(g, lax.rem(t + i, N_T)), device_id_type=MESH
-        )
-        return c
-
-    lax.fori_loop(1, N_T, greet, 0)
-    for i in range(1, N_G):
-        pl.semaphore_signal(
-            barrier, inc=1, device_id=(lax.rem(g + i, N_G), t), device_id_type=MESH
-        )
+    near = [(g, idx(1 - xh, y, z))]
+    near += [(g, idx(xh, y + d, z)) for d in (1, -1)]
+    near += [(g, idx(xh, y, z + d)) for d in (1, -1)]
+    near += [(lax.rem(g + i, N_G), t) for i in range(1, N_G)]
+    for to in near:
+        pl.semaphore_signal(barrier, inc=1, device_id=to, device_id_type=MESH)
 
     loads = [
         pltpu.make_async_copy(wqkv_hbm, wq, load_sem.at[0]),
@@ -56,22 +51,26 @@
     for c in loads:
         c.start()
 
-    for s in range(N_G):
-        rows = tok[s].astype(F32)
+    for j in range(3):
+        rows = tok[j].astype(F32)
         mean = jnp.mean(rows * rows, axis=-1, keepdims=True)
         normed = rows * lax.rsqrt(mean + EPS) * gain[...]
-        for q in range(4):
-            stage[s, 4 * q : 4 * q + 3, :] = normed[:, q * QW : (q + 1) * QW]
-        for c in range(12):
-            at = MAIN + (c % 4) * CHUNK
-            lane = (c % 3) * CHUNK
-            row = 4 * (c // 3) + 3
-            stage[s, row : row + 1, lane : lane + CHUNK] = normed[
-                c // 4 : c // 4 + 1, at : at + CHUNK
-            ]
+        for s in range(N_G):
+            for q in range(4):
+                stage[s, 4 * q + j : 4 * q + j + 1, :] = normed[
+                    s : s + 1, q * QW : (q + 1) * QW
+                ]
+            for c in range(4 * j, 4 * j + 4):
+                at = MAIN + (c % 4) * CHUNK
+                lane = (c % 3) * CHUNK
+                row = 4 * (c // 3) + 3
+                stage[s, row : row + 1, lane : lane + CHUNK] = normed[
+                    s : s + 1, at : at + CHUNK
+                ]
+    for s in range(N_G):
         gsend[s] = stage[s].astype(BF16)
 
-    pl.semaphore_wait(barrier, N_T - 1 + N_G - 1)
+    pl.semaphore_wait(barrier, len(near))
 
     def group_exchange(src, dst, base):
         copies = []
@@ -192,7 +191,9 @@
             return xg[q, pl.ds(xx * 16, 16), :, a:b].reshape(256, b - a)
 
         def dot(l, a, b):
-            return jnp.dot(l, wq[a:b, :], preferred_element_type=F32)
+            return lax.dot_general(
+                l, wq[:, a:b], (((1,), (1,)), ((), ())), preferred_element_type=F32
+            )
 
         m = MAIN
         main = dot(lhs(0), 0, QW)
@@ -521,16 +522,20 @@
     sent.extend(group_exchange(fsend, frecv, N_G))
     for s in range(N_G):
         stage[s] = frecv[s].astype(F32)
-        for q in range(4):
-            o32[s, :, q * QW : (q + 1) * QW] = stage[s, 4 * q : 4 * q + 3, :]
-        for c in range(12):
-            at = MAIN + (c % 4) * CHUNK
-            lane = (c % 3) * CHUNK
-            row = 4 * (c // 3) + 3
-            o32[s, c // 4 : c // 4 + 1, at : at + CHUNK] = stage[
-                s, row : row + 1, lane : lane + CHUNK
-            ]
-        out[s] = (tok[s].astype(F32) + o32[s]).astype(BF16)
+        for j in range(3):
+            for q in range(4):
+                o32[j, s : s + 1, q * QW : (q + 1) * QW] = stage[
+                    s, 4 * q + j : 4 * q + j + 1, :
+                ]
+            for c in range(4 * j, 4 * j + 4):
+                at = MAIN + (c % 4) * CHUNK
+                lane = (c % 3) * CHUNK
+                row = 4 * (c // 3) + 3
+                o32[j, s : s + 1, at : at + CHUNK] = stage[
+                    s, row : row + 1, lane : lane + CHUNK
+                ]
+    for j in range(3):
+        out[j] = (tok[j].astype(F32) + o32[j]).astype(BF16)
     for c in sent:
         c.wait_send()
 
@@ -543,9 +548,9 @@
     smem = pl.BlockSpec(memory_space=pltpu.SMEM)
     hbm = pl.BlockSpec(memory_space=pl.ANY)
     dma = pltpu.SemaphoreType.DMA
-    return pl.pallas_call(
+    done = pl.pallas_call(
         body,
-        out_shape=jax.ShapeDtypeStruct((4, 3, D), BF16),
+        out_shape=jax.ShapeDtypeStruct((3, 4, D), BF16),
         in_specs=[vmem, vmem, vmem, smem, smem, smem, hbm, hbm, hbm],
         out_specs=vmem,
         scratch_shapes=[
@@ -554,7 +559,7 @@
             pltpu.VMEM((4, 16, QW), BF16),
             pltpu.VMEM((4, 16, QW), F32),
             pltpu.VMEM((4, 32, 16, QW), BF16),
-            pltpu.VMEM((D, 320), BF16),
+            pltpu.VMEM((320, D), BF16),
             pltpu.VMEM((256, D), BF16),
             pltpu.VMEM((12, 2, 8, 128, 128), BF16),
             pltpu.VMEM((256, 384), F32),
@@ -569,7 +574,7 @@
             pltpu.VMEM((4, 16, QW), BF16),
             pltpu.VMEM((4, 16, QW), BF16),
             pltpu.VMEM((4, 16, QW), BF16),
-            pltpu.VMEM((4, 3, D), F32),
+            pltpu.VMEM((3, 4, D), F32),
             dma((3,)),
             dma((2 * N_G,)),
             dma((2 * N_G,)),
@@ -585,9 +590,10 @@
             flops=4 * 10**9, bytes_accessed=17 * 10**6, transcendentals=10**6
         ),
     )(
-        tokens, norm_gain.reshape(1, D), inverse, lengths, migrate, page_order,
-        w_qkv, w_out, kv_pool.reshape(12, 2, 8, 128, 128),
+        tokens.transpose(1, 0, 2), norm_gain.reshape(1, D), inverse, lengths, migrate, page_order,
+        w_qkv.T, w_out, kv_pool.reshape(12, 2, 8, 128, 128),
     )
+    return done.transpose(1, 0, 2)
 
 
 def solution(mesh):

time: 138 us -> 124 us (0.90)
  local copies, waits for them, and re-layouts: 11.8 us -> 1.67 us
  Pallas kernels: 124 us -> 120 us
    unnamed x2 -> x1, local copies, waits for them, and re-layouts: 9.99 us -> 1.67 us
    pallas_call x1, Pallas kernels: 124 us -> 120 us  [per_device(): pl.pallas_call(body, out_shape=jax.ShapeDtypeStruct((3, 4, D), BF16), in_...]
    pallas_call x1 -> x0, local copies, waits for them, and re-layouts: 1.81 us -> none  [per_device(): pl.pallas_call(body, out_shape=jax.ShapeDtypeStruct((4, 3, D), BF16), in_...]
where the time goes in v2:
time: 124 us; the launch traced here: 122 us
  Pallas kernels  120 us (97%)
  local copies, waits for them, and re-layouts  1.67 us (1%)
    pallas_call x1, Pallas kernels, per_device(): pl.pallas_call(body, out_shape=jax.ShapeDtypeStruct((3, 4, D), BF16), in_...  120 us

profile of v2, /device:TPU:1, one launch (start us, length us, event | category | flops | bytes accessed | tf_op | source)
XLA Modules:
  0.0 122.3 jit_solution(10698036377490387514)
XLA Ops:
  0.0 0.6 maximum_bitcast_fusion.inv
  0.6 120.0 %shard_map.91 = bf16[3,4,8192]{2,1,0:T(4,128)(2,1)} custom-call(bf16[3,4,8192]{2,1,0:T(4,128)(2,1)} %bitcast.10, f32[1,8192]{1,0:T(1,128)} %bitcast.11, f32[1,128]{1,0:T(1,128)} %maximum_bitcast_fusion.inv, s32[1,4]{1,0:T(1,128)} %lens.1, s32[1,4]{1,0:T(1,128)} %mig.1, s32[1,12]{1,0:T(1,128)} %order.1, bf16[320,8192]{1,0:T(8,128)(2,1)} %bitcast.8, ...), custom_call_target="tpu_custom_call" | custom-call | flops 4000000000 | bytes 17000000 | tf_op jit(solution)/shard_map/pallas_call | solution.py:551
  120.7 1.7 %copy.11 = bf16[4,3,8192]{2,0,1:T(4,128)(2,1)} copy(bf16[4,3,8192]{2,0,1:T(4,128)(2,1)} %bitcast.9) | data formatting | bytes 393216
  (1 shorter events, 0.0 us)

commit v3 on v2

--- a/solution.py
+++ b/solution.py
@@ -17,14 +17,15 @@
 MAIN = 6144
 QW = 1536
 CHUNK = 512
+LX = 256
 N_T = 32
 N_G = 4
 
 
 def body(
-    tok, gain, inv, lens, mig, order, wqkv_hbm, wout_hbm, kv_hbm, out,
-    stage, gsend, grecv, x32, xg, wq, wo, kv, qacc, qout, qin, heads, att, ain,
-    terms, rq, rf, rx, fsend, frecv, o32,
+    gain, inv, lens, mig, order, tok_hbm, wqkv_hbm, wout_hbm, kv_hbm, out,
+    tok, stage, gsend, grecv, x32, xg, wq, wo, kv, qacc, qout, qin, heads, att, ain,
+    terms, rq, rf, rx, rc, fsend, frecv, o32,
     load_sem, gs_sem, gr_sem, s_sem, r_sem, as_sem, ar_sem,
 ):
     g = lax.axis_index("group")
@@ -34,7 +35,12 @@
     def idx(xx, yy, zz):
         return xx * 16 + lax.rem(yy + 4, 4) * 4 + lax.rem(zz + 4, 4)
 
+    def spot(xx, yy, zz):
+        return xx, lax.rem(yy + 4, 4), lax.rem(zz + 4, 4)
+
     barrier = pltpu.get_barrier_semaphore()
+    first_load = pltpu.make_async_copy(tok_hbm, tok, load_sem.at[3])
+    first_load.start()
 
     near = [(g, idx(1 - xh, y, z))]
     near += [(g, idx(xh, y + d, z)) for d in (1, -1)]
@@ -51,6 +57,7 @@
     for c in loads:
         c.start()
 
+    first_load.wait()
     for j in range(3):
         rows = tok[j].astype(F32)
         mean = jnp.mean(rows * rows, axis=-1, keepdims=True)
@@ -96,7 +103,7 @@
         for q in range(4):
             x32[q, 4 * gg : 4 * gg + 4, :] = stage[gg, 4 * q : 4 * q + 4, :]
     for q in range(4):
-        xg[q, t] = x32[q].astype(BF16)
+        xg[q, xh, y, z] = x32[q].astype(BF16)
 
     def send(src, dst, k, to):
         c = pltpu.make_async_remote_copy(
@@ -108,22 +115,28 @@
         return c
 
     class Gather:
-        def __init__(self, at, q, k):
-            self.at, self.q, self.k, self.to = at[0], q, k, at[1]
+        def __init__(self, at, q, k, lanes):
+            (self.at, self.to), self.q, self.k = at, q, k
+            self.lanes = slice(0, lanes)
+
+        def block(self, o, one=None):
+            if one is None:
+                return xg.at[(pl.ds(self.q, 2), *self.at(o), slice(None), self.lanes)]
+            return xg.at[(self.q + one, *self.at(o), slice(None), self.lanes)]
 
         def start(self):
-            ref = xg.at[pl.ds(self.q, 2), self.at(0)]
+            ref = self.block(0)
             self.up = send(ref, ref, self.k, self.to(1))
             self.down = send(ref, ref, self.k + 1, self.to(-1))
 
         def mid_up(self):
             self.up.wait_recv()
-            ref = xg.at[self.q, self.at(-1)]
+            ref = self.block(-1, 0)
             self.up2 = send(ref, ref, self.k + 2, self.to(1))
 
         def mid_down(self):
             self.down.wait_recv()
-            ref = xg.at[self.q + 1, self.at(1)]
+            ref = self.block(1, 1)
             self.down2 = send(ref, ref, self.k + 3, self.to(-1))
 
         def mid(self):
@@ -134,24 +147,39 @@
             self.up2.wait_recv()
             self.down2.wait_recv()
 
-    def place(half, xx, first, second):
-        return idx(xx, y + first, z + second) if half == 0 else idx(xx, y + second, z + first)
+    def place(make, half, xx, first, second):
+        return make(xx, y + first, z + second) if half == 0 else make(xx, y + second, z + first)
 
     def ring_first(half, xx):
-        return (lambda o: place(half, xx, o, 0)), (lambda o: place(half, xh, o, 0))
+        return (
+            lambda o: place(spot, half, xx, o, 0),
+            lambda o: place(idx, half, xh, o, 0),
+        )
 
     def ring_second(half, xx, e):
-        return (lambda o: place(half, xx, e, o)), (lambda o: place(half, xh, 0, o))
+        return (
+            lambda o: place(spot, half, xx, e, o),
+            lambda o: place(idx, half, xh, 0, o),
+        )
+
+    def line(half, xx, e):
+        _, yy, zz = place(spot, half, xx, e, 0)
+        return (xx, yy, slice(None)) if half == 0 else (xx, slice(None), zz)
 
     OFFS = (0, -1, 1, 2)
     own, peer = xh, 1 - xh
 
     class GatherSet:
         def __init__(self, xx, n):
-            self.one = [Gather(ring_first(h, xx), 2 * h, 40 * n + 20 * h) for h in (0, 1)]
+            lanes = QW if n == 0 else QW - LX
+            self.one = [
+                Gather(ring_first(h, xx), 2 * h, 40 * n + 20 * h, lanes) for h in (0, 1)
+            ]
             self.two = [
                 {
-                    e: Gather(ring_second(h, xx, e), 2 * h, 40 * n + 20 * h + 4 + 4 * i)
+                    e: Gather(
+                        ring_second(h, xx, e), 2 * h, 40 * n + 20 * h + 4 + 4 * i, lanes
+                    )
                     for i, e in enumerate(OFFS)
                 }
                 for h in (0, 1)
@@ -188,7 +216,7 @@
 
     def project(xx):
         def lhs(q, a=0, b=QW):
-            return xg[q, pl.ds(xx * 16, 16), :, a:b].reshape(256, b - a)
+            return xg[q, xx, :, :, :, a:b].reshape(256, b - a)
 
         def dot(l, a, b):
             return lax.dot_general(
@@ -208,11 +236,19 @@
         for s in range(3):
             qacc[:, 0:320] = tails[s]
             add = jnp.where(row16 == s, pltpu.roll(qacc[...], 256 - (3 - s), 0)[:, 0:320], add)
-        qacc[:, 0:320] = jnp.where(row16 == 3, 0.0, main + add)
+        qacc[:, 0:320] = main + add
         qacc[:, 320:384] = jnp.zeros((256, 64), F32)
         flat = qacc[...]
-        flat = jnp.where(lax.rem(t, 2) == 1, pltpu.roll(flat, 64, 1), flat)
-        qout[pl.ds(xx * 16, 16)] = flat.reshape(16, 16, 384).astype(BF16)
+        odd = lax.rem(t, 2) == 1
+        full = jnp.where(odd, pltpu.roll(flat, 320, 1)[:, 0:256], flat[:, 0:256])
+        part = jnp.where(odd, flat[:, 0:128], flat[:, 256:384])
+        lane = lax.broadcasted_iota(jnp.int32, (256, 128), 1)
+        left = jnp.where(
+            lane < 64, pltpu.roll(part, 3, 0), pltpu.roll(pltpu.roll(part, 2, 0), 64, 1)
+        )
+        right = pltpu.roll(part, 1, 0)
+        both = jnp.where(row16 == 3, jnp.concatenate([left, right], axis=1), full)
+        qout[pl.ds(xx * 16, 16)] = both.reshape(16, 16, 256).astype(BF16)
 
     def a2a(src, dst, base, to):
         return pltpu.make_async_remote_copy(
@@ -236,20 +272,30 @@
         lax.fori_loop(1, N_T, one, 0)
 
     near_set, far_set = GatherSet(own, 0), GatherSet(peer, 1)
+
+    def across(e):
+        got = []
+        for h in (0, 1):
+            near_set.two[h][e].end()
+            ref = xg.at[(pl.ds(2 * h, 2), *line(h, own, e), slice(None), pl.ds(QW - LX, LX))]
+            got.append(send(ref, ref, 242 + 2 * OFFS.index(e) + h, far))
+        return got
+
     near_set.s1()
-    whole = xg.at[:, t]
-    across = send(whole, whole, 160, far)
+    mine = xg.at[:, xh, y, z, :, 0 : QW - LX]
+    over = [send(mine, mine, 160, far)]
     near_set.s2()
     near_set.mid(0)
     near_set.s4()
-    across.wait_recv()
+    over[0].wait_recv()
     far_set.s1()
     near_set.mid(-1)
     near_set.mid(1)
+    over += across(0)
     far_set.s2()
     near_set.mid(2)
-    for e in OFFS:
-        near_set.end(e)
+    for e in (-1, 1, 2):
+        over += across(e)
     far_set.mid(0)
     far_set.s4()
     far_set.mid(-1)
@@ -267,6 +313,8 @@
     far_set.mid(2)
     for e in OFFS:
         far_set.end(e)
+    for c in over[1:]:
+        c.wait_recv()
     project(peer)
 
     def send_far(i, c):
@@ -305,13 +353,18 @@
 
     a2a_wait(qout, qin, 0)
 
+    def unpack(block):
+        one, two = block[:, 0:128], block[:, 128:256]
+        step = r16 & 3
+        half = jnp.where(
+            step == 0, pltpu.roll(one, 13, 0), pltpu.roll(pltpu.roll(one, 14, 0), 64, 1)
+        )
+        return one, two, jnp.where(step == 2, pltpu.roll(two, 15, 0), half)
+
     def pair(p, c):
-        even, odd = qin[2 * p].astype(F32), qin[2 * p + 1].astype(F32)
-        five = (
-            even[:, 0:128], even[:, 128:256],
-            jnp.where(lane16 < 64, even[:, 256:384], odd[:, 0:128]),
-            odd[:, 128:256], odd[:, 256:384],
-        )
+        e0, e1, low = unpack(qin[2 * p].astype(F32))
+        o0, o1, high = unpack(qin[2 * p + 1].astype(F32))
+        five = (e0, e1, jnp.where(lane16 < 64, low, pltpu.roll(high, 64, 1)), o0, o1)
         for i, h in enumerate(five):
             turned = h * cosine + pltpu.roll(h, 64, 1) * sine
             heads[5 * p + i] = jnp.where(5 * p + i < 72, turned, h).astype(BF16)
@@ -322,7 +375,9 @@
     loads[1].wait()
     r128 = lax.broadcasted_iota(jnp.int32, (128, 128), 0)
     c128 = lax.broadcasted_iota(jnp.int32, (128, 128), 1)
-    lim = by_row(r128, row_len)
+    r512 = lax.broadcasted_iota(jnp.int32, (128, 512), 0)
+    c512 = lax.broadcasted_iota(jnp.int32, (128, 512), 1)
+    lim = by_row(lax.broadcasted_iota(jnp.int32, (128, 1), 0), row_len)
     fresh = (
         (c128 < 16) & ((c128 >> 2) == ((r128 & 15) >> 2)) & ((c128 & 3) <= (r128 & 3))
     )
@@ -336,36 +391,39 @@
                 queries, keys, (((1,), (1,)), ((), ())), preferred_element_type=F32
             )
 
-        blocks, masks = [], []
-        for b in range(4):
-            blocks.append(
-                by_row(r128, [scores(kv[pages[gg][b], 0, k]) for gg in range(N_G)]) * SCALE
+        def page(gg, b, what):
+            return kv[pages[gg][b], what, k]
+
+        cached = [
+            scores(jnp.concatenate([page(gg, b, 0) for b in range(4)], axis=0))
+            for gg in range(N_G)
+        ]
+        cached = by_row(r512, cached) * SCALE
+        live = c512 < lim
+        cached = jnp.where(live, cached, NEG_FILL)
+        newest = scores(jnp.concatenate([heads[64 + k], pad], axis=0)) * SCALE
+        newest = jnp.where(fresh, newest, NEG_FILL)
+        top = jnp.maximum(
+            jnp.max(cached, axis=-1, keepdims=True), jnp.max(newest, axis=-1, keepdims=True)
+        )
+        weights = jnp.where(live, jnp.exp(cached - top), 0.0).astype(BF16)
+        extra = jnp.where(fresh, jnp.exp(newest - top), 0.0).astype(BF16)
+        total = jnp.sum(weights.astype(F32), axis=-1, keepdims=True) + jnp.sum(
+            extra.astype(F32), axis=-1, keepdims=True
+        )
+        acc = []
+        for pair_of in ((0, 1), (2, 3)):
+            values = jnp.concatenate(
+                [
+                    jnp.concatenate([page(gg, b, 1) for b in range(4)], axis=0)
+                    for gg in pair_of
+                ],
+                axis=1,
             )
-            masks.append(c128 + b * 128 < lim)
-        blocks.append(scores(jnp.concatenate([heads[64 + k], pad], axis=0)) * SCALE)
-        masks.append(fresh)
-        tops = [jnp.where(m, s, NEG_FILL) for m, s in zip(masks, blocks)]
-        top = tops[0]
-        for s in tops[1:]:
-            top = jnp.maximum(top, s)
-        top = jnp.max(top, axis=-1, keepdims=True)
-        weights = [
-            jnp.where(m, jnp.exp(s - top), 0.0).astype(BF16) for m, s in zip(masks, tops)
-        ]
-        total = weights[0].astype(F32)
-        for w in weights[1:]:
-            total = total + w.astype(F32)
-        total = jnp.sum(total, axis=-1, keepdims=True)
-        acc = []
-        for gg in range(N_G):
-            a = jnp.dot(weights[0], kv[pages[gg][0], 1, k], preferred_element_type=F32)
-            for b in (1, 2, 3):
-                a = a + jnp.dot(
-                    weights[b], kv[pages[gg][b], 1, k], preferred_element_type=F32
-                )
-            acc.append(a)
+            two = jnp.dot(weights, values, preferred_element_type=F32)
+            acc += [two[:, 0:128], two[:, 128:256]]
         acc = by_row(r128, acc) + jnp.dot(
-            weights[4],
+            extra,
             jnp.concatenate([heads[72 + k], pad], axis=0),
             preferred_element_type=F32,
         )
@@ -383,7 +441,7 @@
         lax.fori_loop(0, 4, give, 0)
         return c
 
-    lax.fori_loop(0, 8, attend, 0)
+    lax.fori_loop(0, 8, attend, 0, unroll=2)
     ain[t] = att[t]
     loads[2].wait()
     a2a_wait(att, ain, N_T)
@@ -404,61 +462,73 @@
             )
             tail = jnp.dot(turned[c // 4], wo[:, at : at + CHUNK], preferred_element_type=F32)
             lane = (c % 3) * CHUNK
-            terms[c // 3, pl.ds(xx * 16, 16), :, lane : lane + CHUNK] = (
-                jnp.where(row16 == 3, tail, main).reshape(16, 16, CHUNK).astype(BF16)
+            terms[c // 3, xx, :, :, :, lane : lane + CHUNK] = (
+                jnp.where(row16 == 3, tail, main).reshape(4, 4, 16, CHUNK).astype(BF16)
             )
 
     class Reduce:
-        def __init__(self, at, q, k, n):
+        def __init__(self, at, q, k, n, lanes):
             self.at, self.to = at
             self.q, self.k, self.n = q, k, n
+            self.lanes = slice(0, lanes)
+
+        def part(self, o, i):
+            return (self.q + i, *self.at(o), slice(None), self.lanes)
+
+        def both(self, o):
+            return (pl.ds(self.q, 2), *self.at(o), slice(None), self.lanes)
 
         def s1(self):
-            q, k, n = self.q, self.k, self.n
-            self.up = send(terms.at[q, self.at(2)], rq.at[n, 0], k, self.to(1))
-            self.down = send(terms.at[q + 1, self.at(-2)], rq.at[n, 1], k + 1, self.to(-1))
+            k, n, w = self.k, self.n, self.lanes
+            self.up = send(terms.at[self.part(2, 0)], rq.at[n, 0, :, w], k, self.to(1))
+            self.down = send(terms.at[self.part(-2, 1)], rq.at[n, 1, :, w], k + 1, self.to(-1))
 
         def s2(self):
-            q, k, n = self.q, self.k, self.n
-            self.up.wait_recv()
-            a = self.at(1)
-            terms[q, a] = (terms[q, a].astype(F32) + rq[n, 0].astype(F32)).astype(BF16)
-            self.up2 = send(terms.at[pl.ds(q, 2), a], rf.at[n, 0], k + 2, self.to(1))
-            self.down.wait_recv()
-            b = self.at(-1)
-            terms[q + 1, b] = (terms[q + 1, b].astype(F32) + rq[n, 1].astype(F32)).astype(BF16)
-            self.down2 = send(terms.at[pl.ds(q, 2), b], rf.at[n, 1], k + 3, self.to(-1))
+            k, n, w = self.k, self.n, self.lanes
+            for i, d, came in ((0, 1, self.up), (1, -1, self.down)):
+                came.wait_recv()
+                p = self.part(d, i)
+                terms[p] = (terms[p].astype(F32) + rq[n, i, :, w].astype(F32)).astype(BF16)
+                on = send(
+                    terms.at[self.both(d)], rf.at[n, i, :, :, w], k + 2 + i, self.to(d)
+                )
+                if i == 0:
+                    self.up2 = on
+                else:
+                    self.down2 = on
 
         def s3(self):
-            q, n = self.q, self.n
+            n, w = self.n, self.lanes
             self.up2.wait_recv()
             self.down2.wait_recv()
-            a = self.at(0)
             for i in (0, 1):
-                terms[q + i, a] = (
-                    terms[q + i, a].astype(F32)
-                    + rf[n, 0, i].astype(F32)
-                    + rf[n, 1, i].astype(F32)
+                p = self.part(0, i)
+                terms[p] = (
+                    terms[p].astype(F32)
+                    + rf[n, 0, i, :, w].astype(F32)
+                    + rf[n, 1, i, :, w].astype(F32)
                 ).astype(BF16)
 
     class ReduceSet:
         def __init__(self, xx, n):
             k, m = 161 + 40 * n, 10 * n
+            lanes = QW - LX if n == 0 else QW
             self.big = [
                 {
                     e: Reduce(
-                        ring_second(h, xx, e), 2 * h, k + 20 * h + 4 * i, m + 5 * h + i
+                        ring_second(h, xx, e), 2 * h, k + 20 * h + 4 * i, m + 5 * h + i, lanes
                     )
                     for i, e in enumerate(OFFS)
                 }
                 for h in (0, 1)
             ]
             self.last = [
-                Reduce(ring_first(h, xx), 2 * h, k + 20 * h + 16, m + 5 * h + 4) for h in (0, 1)
+                Reduce(ring_first(h, xx), 2 * h, k + 20 * h + 16, m + 5 * h + 4, lanes)
+                for h in (0, 1)
             ]
 
-        def s1(self, h):
-            for e in (2, -1, 1, 0):
+        def s1(self, h, *es):
+            for e in es:
                 self.big[h][e].s1()
 
         def s2(self, *es):
@@ -484,36 +554,71 @@
                 self.last[h].s3()
 
     far_sum, near_sum = ReduceSet(peer, 0), ReduceSet(own, 1)
+    BACK = (2, -1, 1, 0)
+    cross = {}
+
+    def hand(h):
+        for i, e in enumerate(BACK):
+            lanes = pl.ds(QW - LX, LX)
+            _, yy, zz = line(h, peer, e)
+            cross[h, e] = send(
+                terms.at[pl.ds(2 * h, 2), peer, yy, zz, :, lanes],
+                rc.at[pl.ds(2 * h, 2), yy, zz],
+                250 + 4 * h + i,
+                far,
+            )
+
+    def take(h, e):
+        cross[h, e].wait_recv()
+        for q in (2 * h, 2 * h + 1):
+            for o in range(4):
+                _, yy, zz = place(spot, h, own, e, o)
+                old = terms[q, own, yy, zz, :, QW - LX : QW].astype(F32)
+                terms[q, own, yy, zz, :, QW - LX : QW] = (
+                    old + rc[q, yy, zz].astype(F32)
+                ).astype(BF16)
+        near_sum.s1(h, e)
+
     sides = lhs_of(peer)
     expand(sides, peer, 0)
-    far_sum.s1(0)
+    far_sum.s1(0, *BACK)
+    hand(0)
     expand(sides, peer, 1)
-    far_sum.s1(1)
-    far_sum.s2(2, -1, 1, 0)
+    far_sum.s1(1, *BACK)
+    hand(1)
+    far_sum.s2(*BACK)
     sides = lhs_of(own)
     expand(sides, own, 0)
-    near_sum.s1(0)
     expand(sides, own, 1)
-    near_sum.s1(1)
+    take(0, 2)
+    take(1, 2)
     far_sum.s3(2)
     far_sum.l1()
+    take(0, -1)
+    take(1, -1)
     near_sum.s2(2)
     far_sum.s3(-1, 1)
     far_sum.l2()
-    near_sum.s2(-1, 1)
+    take(0, 1)
+    take(1, 1)
+    near_sum.s2(-1)
     far_sum.s3(0)
     far_sum.l3()
-    over = send(terms.at[:, far], rx, 241, far)
-    near_sum.s2(0)
+    over = send(terms.at[:, peer, y, z, :, 0 : QW - LX], rx, 241, far)
+    take(0, 0)
+    take(1, 0)
+    near_sum.s2(1)
     near_sum.s3(2)
     near_sum.l1()
+    near_sum.s2(0)
     near_sum.s3(-1, 1)
     near_sum.l2()
     near_sum.s3(0)
     near_sum.l3()
     over.wait_recv()
     for q in range(4):
-        x32[q] = terms[q, t].astype(F32) + rx[q].astype(F32)
+        x32[q, :, 0 : QW - LX] = terms[q, xh, y, z, :, 0 : QW - LX].astype(F32) + rx[q].astype(F32)
+        x32[q, :, QW - LX : QW] = terms[q, xh, y, z, :, QW - LX : QW].astype(F32)
     for gg in range(N_G):
         for q in range(4):
             stage[gg, 4 * q : 4 * q + 4, :] = x32[q, 4 * gg : 4 * gg + 4, :]
@@ -535,15 +640,14 @@
                     s, row : row + 1, lane : lane + CHUNK
                 ]
     for j in range(3):
-        out[j] = (tok[j].astype(F32) + o32[j]).astype(BF16)
+        out[j] = o32[j].astype(BF16)
     for c in sent:
         c.wait_send()
 
 
 def per_device(tokens, norm_gain, w_qkv, w_out, lengths, migrate, page_order, kv_pool):
-    half = np.arange(64, dtype=np.float32)
-    inverse = jnp.float32(ROPE_BASE) ** (-(jnp.asarray(half) * 2.0 / 128))
-    inverse = jnp.concatenate([inverse, inverse]).reshape(1, 128)
+    inverse = np.float32(ROPE_BASE) ** (-(np.arange(64, dtype=np.float32) * np.float32(2.0) / 128))
+    inverse = jnp.asarray(np.concatenate([inverse, inverse]).reshape(1, 128), F32)
     vmem = pl.BlockSpec(memory_space=pltpu.VMEM)
     smem = pl.BlockSpec(memory_space=pltpu.SMEM)
     hbm = pl.BlockSpec(memory_space=pl.ANY)
@@ -551,35 +655,37 @@
     done = pl.pallas_call(
         body,
         out_shape=jax.ShapeDtypeStruct((3, 4, D), BF16),
-        in_specs=[vmem, vmem, vmem, smem, smem, smem, hbm, hbm, hbm],
+        in_specs=[vmem, vmem, smem, smem, smem, hbm, hbm, hbm, hbm],
         out_specs=vmem,
         scratch_shapes=[
+            pltpu.VMEM((3, 4, D), BF16),
             pltpu.VMEM((4, 16, QW), F32),
             pltpu.VMEM((4, 16, QW), BF16),
             pltpu.VMEM((4, 16, QW), BF16),
             pltpu.VMEM((4, 16, QW), F32),
-            pltpu.VMEM((4, 32, 16, QW), BF16),
+            pltpu.VMEM((4, 2, 4, 4, 16, QW), BF16),
             pltpu.VMEM((320, D), BF16),
             pltpu.VMEM((256, D), BF16),
             pltpu.VMEM((12, 2, 8, 128, 128), BF16),
             pltpu.VMEM((256, 384), F32),
-            pltpu.VMEM((32, 16, 384), BF16),
-            pltpu.VMEM((32, 16, 384), BF16),
+            pltpu.VMEM((32, 16, 256), BF16),
+            pltpu.VMEM((32, 16, 256), BF16),
             pltpu.VMEM((80, 16, 128), BF16),
             pltpu.VMEM((32, 2, 16, 128), BF16),
             pltpu.VMEM((32, 2, 16, 128), BF16),
-            pltpu.VMEM((4, 32, 16, QW), BF16),
+            pltpu.VMEM((4, 2, 4, 4, 16, QW), BF16),
             pltpu.VMEM((20, 2, 16, QW), BF16),
             pltpu.VMEM((20, 2, 2, 16, QW), BF16),
-            pltpu.VMEM((4, 16, QW), BF16),
+            pltpu.VMEM((4, 16, QW - LX), BF16),
+            pltpu.VMEM((4, 4, 4, 16, LX), BF16),
             pltpu.VMEM((4, 16, QW), BF16),
             pltpu.VMEM((4, 16, QW), BF16),
             pltpu.VMEM((3, 4, D), F32),
-            dma((3,)),
+            dma((4,)),
             dma((2 * N_G,)),
             dma((2 * N_G,)),
-            dma((242,)),
-            dma((242,)),
+            dma((258,)),
+            dma((258,)),
             dma((2 * N_T,)),
             dma((2 * N_T,)),
         ],
@@ -590,10 +696,10 @@
             flops=4 * 10**9, bytes_accessed=17 * 10**6, transcendentals=10**6
         ),
     )(
-        tokens.transpose(1, 0, 2), norm_gain.reshape(1, D), inverse, lengths, migrate, page_order,
-        w_qkv.T, w_out, kv_pool.reshape(12, 2, 8, 128, 128),
+        norm_gain.reshape(1, D), inverse, lengths, migrate, page_order,
+        tokens.transpose(1, 0, 2), w_qkv.T, w_out, kv_pool.reshape(12, 2, 8, 128, 128),
     )
-    return done.transpose(1, 0, 2)
+    return (tokens.astype(F32) + done.transpose(1, 0, 2).astype(F32)).astype(BF16)
 
 
 def solution(mesh):

time: 124 us -> 116 us (0.935); the launches traced: 122 us -> 116 us
  Pallas kernels: 120 us -> 115 us
  local copies, waits for them, and re-layouts: 1.67 us -> 0.01 us
    pallas_call x1, Pallas kernels: 120 us -> 115 us  [per_device(): pl.pallas_call(body, out_shape=jax.ShapeDtypeStruct((3, 4, D), BF16), in_...]
    convert_element_type x0 -> x1, other arithmetic: none -> 1.71 us  [per_device(): (tokens.astype(F32) + done.transpose(1, 0, 2).astype(F32)).astype(BF16)]
    unnamed x1 -> x2, local copies, waits for them, and re-layouts: 1.67 us -> 0.01 us
where the time goes in v3:
time: 116 us
  Pallas kernels  115 us (99%)
  other arithmetic  1.71 us (1%)
    pallas_call x1, Pallas kernels, per_device(): pl.pallas_call(body, out_shape=jax.ShapeDtypeStruct((3, 4, D), BF16), in_...  115 us

profile of v3, /device:TPU:1, one launch (start us, length us, event | category | flops | bytes accessed | tf_op | source)
XLA Modules:
  0.0 116.3 jit_solution(15436270047088730107)
XLA Ops:
  0.0 0.0 copy-start
  0.0 114.5 %shard_map.91 = bf16[3,4,8192]{2,1,0:T(4,128)(2,1)} custom-call(f32[1,8192]{1,0:T(1,128)} %bitcast.11, f32[1,128]{1,0:T(1,128)} %constant.2.clone.inv, s32[1,4]{1,0:T(1,128)} %lens.1, s32[1,4]{1,0:T(1,128)} %mig.1, s32[1,12]{1,0:T(1,128)} %order.1, bf16[3,4,8192]{2,1,0:T(4,128)(2,1)} %bitcast.10, bf16[320,8192]{1,0:T(8,128)(2,1)} %bitcast.9, ...), custom_call_target="tpu_custom_call" | custom-call | flops 4000000000 | bytes 17000000 | tf_op jit(solution)/shard_map/pallas_call | solution.py:655
  114.5 0.0 copy-done
  114.6 1.7 %fusion = bf16[4,3,8192]{2,0,1:T(4,128)(2,1)} fusion(bf16[3,4,8192]{2,1,0:T(4,128)(2,1)} %shard_map.91, bf16[4,3,8192]{2,0,1:T(4,128)(2,1)S(1)} %copy-done), kind=kLoop, calls=%fused_computation.1 | loop fusion | flops 393216 | bytes 589824 | tf_op jit(solution)/shard_map/convert_element_type | solution.py:702
Async XLA Ops:
  0.0 114.5 %copy-start = (bf16[4,3,8192]{2,0,1:T(4,128)(2,1)S(1)}, bf16[4,3,8192]{2,0,1:T(4,128)(2,1)}, u32[]{:S(2)}) copy-start(bf16[4,3,8192]{2,0,1:T(4,128)(2,1)} %param.9) | copy-start | bytes 589828

commit v4 on v3

--- a/solution.py
+++ b/solution.py
@@ -17,7 +17,8 @@
 MAIN = 6144
 QW = 1536
 CHUNK = 512
-LX = 256
+LG = 256
+LR = 256
 N_T = 32
 N_G = 4
 
@@ -171,7 +172,7 @@
 
     class GatherSet:
         def __init__(self, xx, n):
-            lanes = QW if n == 0 else QW - LX
+            lanes = QW if n == 0 else QW - LG
             self.one = [
                 Gather(ring_first(h, xx), 2 * h, 40 * n + 20 * h, lanes) for h in (0, 1)
             ]
@@ -250,26 +251,21 @@
         both = jnp.where(row16 == 3, jnp.concatenate([left, right], axis=1), full)
         qout[pl.ds(xx * 16, 16)] = both.reshape(16, 16, 256).astype(BF16)
 
-    def a2a(src, dst, base, to):
+    def a2a(src, dst, which, to):
         return pltpu.make_async_remote_copy(
             src_ref=src, dst_ref=dst.at[t],
-            send_sem=as_sem.at[base + to], recv_sem=ar_sem.at[base + t],
+            send_sem=as_sem.at[which], recv_sem=ar_sem.at[which],
             device_id=(g, to), device_id_type=MESH,
         )
 
-    def a2a_wait(src, dst, base):
-        def one(i, c):
-            fr = lax.rem(t + i, N_T)
-            d = pltpu.make_async_remote_copy(
-                src_ref=src.at[fr], dst_ref=dst.at[fr],
-                send_sem=as_sem.at[base + fr], recv_sem=ar_sem.at[base + fr],
-                device_id=(g, fr), device_id_type=MESH,
-            )
-            d.wait_recv()
-            d.wait_send()
-            return c
-
-        lax.fori_loop(1, N_T, one, 0)
+    def a2a_wait(src, dst, which):
+        all_of = pltpu.make_async_remote_copy(
+            src_ref=src.at[pl.ds(0, N_T - 1)], dst_ref=dst.at[pl.ds(0, N_T - 1)],
+            send_sem=as_sem.at[which], recv_sem=ar_sem.at[which],
+            device_id=(g, far), device_id_type=MESH,
+        )
+        all_of.wait_recv()
+        sent.append(all_of)
 
     near_set, far_set = GatherSet(own, 0), GatherSet(peer, 1)
 
@@ -277,12 +273,12 @@
         got = []
         for h in (0, 1):
             near_set.two[h][e].end()
-            ref = xg.at[(pl.ds(2 * h, 2), *line(h, own, e), slice(None), pl.ds(QW - LX, LX))]
+            ref = xg.at[(pl.ds(2 * h, 2), *line(h, own, e), slice(None), pl.ds(QW - LG, LG))]
             got.append(send(ref, ref, 242 + 2 * OFFS.index(e) + h, far))
         return got
 
     near_set.s1()
-    mine = xg.at[:, xh, y, z, :, 0 : QW - LX]
+    mine = xg.at[:, xh, y, z, :, 0 : QW - LG]
     over = [send(mine, mine, 160, far)]
     near_set.s2()
     near_set.mid(0)
@@ -383,7 +379,8 @@
     )
     pad = jnp.zeros((112, 128), BF16)
 
-    def attend(k, c):
+    def attend(i, c):
+        k = lax.rem(i + 4 * peer, 8)
         queries = heads[pl.ds(8 * k, 8)].reshape(128, 128)
 
         def scores(keys):
@@ -434,7 +431,7 @@
 
             @pl.when(to != t)
             def _():
-                a2a(att.at[to], ain, N_T, to).start()
+                a2a(att.at[to], ain, 1, to).start()
 
             return c
 
@@ -444,7 +441,7 @@
     lax.fori_loop(0, 8, attend, 0, unroll=2)
     ain[t] = att[t]
     loads[2].wait()
-    a2a_wait(att, ain, N_T)
+    a2a_wait(att, ain, 1)
 
     def lhs_of(xx):
         left = jnp.concatenate(
@@ -453,9 +450,9 @@
         wide = left.astype(F32)
         return left, [pltpu.roll(wide, 3 - s, 0).astype(BF16) for s in range(3)]
 
-    def expand(sides, xx, half):
+    def expand(sides, xx, q):
         left, turned = sides
-        for c in range(6 * half, 6 * half + 6):
+        for c in range(3 * q, 3 * q + 3):
             at = MAIN + (c % 4) * CHUNK
             main = jnp.dot(
                 left, wo[:, c * CHUNK : (c + 1) * CHUNK], preferred_element_type=F32
@@ -478,10 +475,14 @@
         def both(self, o):
             return (pl.ds(self.q, 2), *self.at(o), slice(None), self.lanes)
 
-        def s1(self):
+        def s1(self, i):
             k, n, w = self.k, self.n, self.lanes
-            self.up = send(terms.at[self.part(2, 0)], rq.at[n, 0, :, w], k, self.to(1))
-            self.down = send(terms.at[self.part(-2, 1)], rq.at[n, 1, :, w], k + 1, self.to(-1))
+            if i == 0:
+                self.up = send(terms.at[self.part(2, 0)], rq.at[n, 0, :, w], k, self.to(1))
+            else:
+                self.down = send(
+                    terms.at[self.part(-2, 1)], rq.at[n, 1, :, w], k + 1, self.to(-1)
+                )
 
         def s2(self):
             k, n, w = self.k, self.n, self.lanes
@@ -512,7 +513,7 @@
     class ReduceSet:
         def __init__(self, xx, n):
             k, m = 161 + 40 * n, 10 * n
-            lanes = QW - LX if n == 0 else QW
+            lanes = QW - LR if n == 0 else QW
             self.big = [
                 {
                     e: Reduce(
@@ -527,9 +528,9 @@
                 for h in (0, 1)
             ]
 
-        def s1(self, h, *es):
+        def s1(self, h, i, *es):
             for e in es:
-                self.big[h][e].s1()
+                self.big[h][e].s1(i)
 
         def s2(self, *es):
             for e in es:
@@ -543,7 +544,8 @@
 
         def l1(self):
             for h in (0, 1):
-                self.last[h].s1()
+                self.last[h].s1(0)
+                self.last[h].s1(1)
 
         def l2(self):
             for h in (0, 1):
@@ -559,7 +561,7 @@
 
     def hand(h):
         for i, e in enumerate(BACK):
-            lanes = pl.ds(QW - LX, LX)
+            lanes = pl.ds(QW - LR, LR)
             _, yy, zz = line(h, peer, e)
             cross[h, e] = send(
                 terms.at[pl.ds(2 * h, 2), peer, yy, zz, :, lanes],
@@ -573,23 +575,23 @@
         for q in (2 * h, 2 * h + 1):
             for o in range(4):
                 _, yy, zz = place(spot, h, own, e, o)
-                old = terms[q, own, yy, zz, :, QW - LX : QW].astype(F32)
-                terms[q, own, yy, zz, :, QW - LX : QW] = (
+                old = terms[q, own, yy, zz, :, QW - LR : QW].astype(F32)
+                terms[q, own, yy, zz, :, QW - LR : QW] = (
                     old + rc[q, yy, zz].astype(F32)
                 ).astype(BF16)
-        near_sum.s1(h, e)
+        near_sum.s1(h, 0, e)
+        near_sum.s1(h, 1, e)
 
     sides = lhs_of(peer)
-    expand(sides, peer, 0)
-    far_sum.s1(0, *BACK)
+    for q in (0, 2, 1, 3):
+        expand(sides, peer, q)
+        far_sum.s1(q // 2, q % 2, *BACK)
     hand(0)
-    expand(sides, peer, 1)
-    far_sum.s1(1, *BACK)
     hand(1)
     far_sum.s2(*BACK)
     sides = lhs_of(own)
-    expand(sides, own, 0)
-    expand(sides, own, 1)
+    for q in range(4):
+        expand(sides, own, q)
     take(0, 2)
     take(1, 2)
     far_sum.s3(2)
@@ -604,7 +606,7 @@
     near_sum.s2(-1)
     far_sum.s3(0)
     far_sum.l3()
-    over = send(terms.at[:, peer, y, z, :, 0 : QW - LX], rx, 241, far)
+    over = send(terms.at[:, peer, y, z, :, 0 : QW - LR], rx, 241, far)
     take(0, 0)
     take(1, 0)
     near_sum.s2(1)
@@ -617,8 +619,8 @@
     near_sum.l3()
     over.wait_recv()
     for q in range(4):
-        x32[q, :, 0 : QW - LX] = terms[q, xh, y, z, :, 0 : QW - LX].astype(F32) + rx[q].astype(F32)
-        x32[q, :, QW - LX : QW] = terms[q, xh, y, z, :, QW - LX : QW].astype(F32)
+        x32[q, :, 0 : QW - LR] = terms[q, xh, y, z, :, 0 : QW - LR].astype(F32) + rx[q].astype(F32)
+        x32[q, :, QW - LR : QW] = terms[q, xh, y, z, :, QW - LR : QW].astype(F32)
     for gg in range(N_G):
         for q in range(4):
             stage[gg, 4 * q : 4 * q + 4, :] = x32[q, 4 * gg : 4 * gg + 4, :]
@@ -676,8 +678,8 @@
             pltpu.VMEM((4, 2, 4, 4, 16, QW), BF16),
             pltpu.VMEM((20, 2, 16, QW), BF16),
             pltpu.VMEM((20, 2, 2, 16, QW), BF16),
-            pltpu.VMEM((4, 16, QW - LX), BF16),
-            pltpu.VMEM((4, 4, 4, 16, LX), BF16),
+            pltpu.VMEM((4, 16, QW - LR), BF16),
+            pltpu.VMEM((4, 4, 4, 16, LR), BF16),
             pltpu.VMEM((4, 16, QW), BF16),
             pltpu.VMEM((4, 16, QW), BF16),
             pltpu.VMEM((3, 4, D), F32),
@@ -686,8 +688,8 @@
             dma((2 * N_G,)),
             dma((258,)),
             dma((258,)),
-            dma((2 * N_T,)),
-            dma((2 * N_T,)),
+            dma((2,)),
+            dma((2,)),
         ],
         compiler_params=pltpu.CompilerParams(
             collective_id=0, has_side_effects=True, vmem_limit_bytes=60 * 2**20

time: 116 us -> 116 us (level)
  no operation moved by 1% of the time
where the time goes in v4:
time: 116 us
  Pallas kernels  114 us (98%)
  other arithmetic  1.71 us (1%)
    pallas_call x1, Pallas kernels, per_device(): pl.pallas_call(body, out_shape=jax.ShapeDtypeStruct((3, 4, D), BF16), in_...  114 us

profile of v4, /device:TPU:1, one launch (start us, length us, event | category | flops | bytes accessed | tf_op | source)
XLA Modules:
  0.0 115.7 jit_solution(1077891515482809739)
XLA Ops:
  0.0 0.0 copy-start
  0.0 113.9 %shard_map.91 = bf16[3,4,8192]{2,1,0:T(4,128)(2,1)} custom-call(f32[1,8192]{1,0:T(1,128)} %bitcast.11, f32[1,128]{1,0:T(1,128)} %constant.2.clone.inv, s32[1,4]{1,0:T(1,128)} %lens.1, s32[1,4]{1,0:T(1,128)} %mig.1, s32[1,12]{1,0:T(1,128)} %order.1, bf16[3,4,8192]{2,1,0:T(4,128)(2,1)} %bitcast.10, bf16[320,8192]{1,0:T(8,128)(2,1)} %bitcast.9, ...), custom_call_target="tpu_custom_call" | custom-call | flops 4000000000 | bytes 17000000 | tf_op jit(solution)/shard_map/pallas_call | solution.py:657
  114.0 0.0 copy-done
  114.0 1.7 %fusion = bf16[4,3,8192]{2,0,1:T(4,128)(2,1)} fusion(bf16[3,4,8192]{2,1,0:T(4,128)(2,1)} %shard_map.91, bf16[4,3,8192]{2,0,1:T(4,128)(2,1)S(1)} %copy-done), kind=kLoop, calls=%fused_computation.1 | loop fusion | flops 393216 | bytes 589824 | tf_op jit(solution)/shard_map/convert_element_type | solution.py:704
Async XLA Ops:
  0.0 114.0 %copy-start = (bf16[4,3,8192]{2,0,1:T(4,128)(2,1)S(1)}, bf16[4,3,8192]{2,0,1:T(4,128)(2,1)}, u32[]{:S(2)}) copy-start(bf16[4,3,8192]{2,0,1:T(4,128)(2,1)} %param.9) | copy-start | bytes 589828

commit v5 on v4

--- a/solution.py
+++ b/solution.py
@@ -24,8 +24,8 @@
 
 
 def body(
-    gain, inv, lens, mig, order, tok_hbm, wqkv_hbm, wout_hbm, kv_hbm, out,
-    tok, stage, gsend, grecv, x32, xg, wq, wo, kv, qacc, qout, qin, heads, att, ain,
+    gain_hbm, inv_hbm, lens_hbm, mig_hbm, order_hbm, tok_hbm, wqkv_hbm, wout_hbm, kv_hbm, out,
+    gain, inv, lens, mig, order, tok, stage, gsend, grecv, x32, xg, wq, wo, kv, qacc, qout, qin, heads, att, ain,
     terms, rq, rf, rx, rc, fsend, frecv, o32,
     load_sem, gs_sem, gr_sem, s_sem, r_sem, as_sem, ar_sem,
 ):
@@ -40,15 +40,24 @@
         return xx, lax.rem(yy + 4, 4), lax.rem(zz + 4, 4)
 
     barrier = pltpu.get_barrier_semaphore()
-    first_load = pltpu.make_async_copy(tok_hbm, tok, load_sem.at[3])
-    first_load.start()
-
     near = [(g, idx(1 - xh, y, z))]
     near += [(g, idx(xh, y + d, z)) for d in (1, -1)]
     near += [(g, idx(xh, y, z + d)) for d in (1, -1)]
     near += [(lax.rem(g + i, N_G), t) for i in range(1, N_G)]
     for to in near:
         pl.semaphore_signal(barrier, inc=1, device_id=to, device_id_type=MESH)
+
+    first_loads = [
+        pltpu.make_async_copy(a, b, load_sem.at[3 + i])
+        for i, (a, b) in enumerate(
+            (
+                (tok_hbm, tok), (gain_hbm, gain), (inv_hbm, inv),
+                (lens_hbm, lens), (mig_hbm, mig), (order_hbm, order),
+            )
+        )
+    ]
+    for c in first_loads:
+        c.start()
 
     loads = [
         pltpu.make_async_copy(wqkv_hbm, wq, load_sem.at[0]),
@@ -58,7 +67,8 @@
     for c in loads:
         c.start()
 
-    first_load.wait()
+    for c in first_loads:
+        c.wait()
     for j in range(3):
         rows = tok[j].astype(F32)
         mean = jnp.mean(rows * rows, axis=-1, keepdims=True)
@@ -651,15 +661,19 @@
     inverse = np.float32(ROPE_BASE) ** (-(np.arange(64, dtype=np.float32) * np.float32(2.0) / 128))
     inverse = jnp.asarray(np.concatenate([inverse, inverse]).reshape(1, 128), F32)
     vmem = pl.BlockSpec(memory_space=pltpu.VMEM)
-    smem = pl.BlockSpec(memory_space=pltpu.SMEM)
     hbm = pl.BlockSpec(memory_space=pl.ANY)
     dma = pltpu.SemaphoreType.DMA
     done = pl.pallas_call(
         body,
         out_shape=jax.ShapeDtypeStruct((3, 4, D), BF16),
-        in_specs=[vmem, vmem, smem, smem, smem, hbm, hbm, hbm, hbm],
+        in_specs=[hbm] * 9,
         out_specs=vmem,
         scratch_shapes=[
+            pltpu.VMEM((1, D), F32),
+            pltpu.VMEM((1, 128), F32),
+            pltpu.SMEM((1, 4), jnp.int32),
+            pltpu.SMEM((1, 4), jnp.int32),
+            pltpu.SMEM((1, 12), jnp.int32),
             pltpu.VMEM((3, 4, D), BF16),
             pltpu.VMEM((4, 16, QW), F32),
             pltpu.VMEM((4, 16, QW), BF16),
@@ -683,7 +697,7 @@
             pltpu.VMEM((4, 16, QW), BF16),
             pltpu.VMEM((4, 16, QW), BF16),
             pltpu.VMEM((3, 4, D), F32),
-            dma((4,)),
+            dma((9,)),
             dma((2 * N_G,)),
             dma((2 * N_G,)),
             dma((258,)),

time: 116 us -> 115 us (level)
  no operation moved by 1% of the time
where the time goes in v5:
time: 115 us
  Pallas kernels  113 us (98%)
  other arithmetic  1.71 us (1%)
    pallas_call x1, Pallas kernels, per_device(): pl.pallas_call(body, out_shape=jax.ShapeDtypeStruct((3, 4, D), BF16), in_...  113 us

profile of v5, /device:TPU:1, one launch (start us, length us, event | category | flops | bytes accessed | tf_op | source)
XLA Modules:
  0.0 114.9 jit_solution(11142969317330915872)
XLA Ops:
  0.0 0.0 copy-start
  0.0 113.1 %shard_map.91 = bf16[3,4,8192]{2,1,0:T(4,128)(2,1)} custom-call(f32[1,8192]{1,0:T(1,128)} %bitcast.11, f32[1,128]{1,0:T(1,128)} %constant.2.clone.inv_hbm, s32[1,4]{1,0:T(1,128)} %lens_hbm.1, s32[1,4]{1,0:T(1,128)} %mig_hbm.1, s32[1,12]{1,0:T(1,128)} %order_hbm.1, bf16[3,4,8192]{2,1,0:T(4,128)(2,1)} %bitcast.10, bf16[320,8192]{1,0:T(8,128)(2,1)} %bitcast.9, ...), custom_call_target="tpu_custom_call" | custom-call | flops 4000000000 | bytes 17000000 | tf_op jit(solution)/shard_map/pallas_call | solution.py:666
  113.1 0.0 copy-done
  113.1 1.7 %fusion = bf16[4,3,8192]{2,0,1:T(4,128)(2,1)} fusion(bf16[3,4,8192]{2,1,0:T(4,128)(2,1)} %shard_map.91, bf16[4,3,8192]{2,0,1:T(4,128)(2,1)S(1)} %copy-done), kind=kLoop, calls=%fused_computation.1 | loop fusion | flops 393216 | bytes 589824 | tf_op jit(solution)/shard_map/convert_element_type | solution.py:718
Async XLA Ops:
  0.0 113.1 %copy-start = (bf16[4,3,8192]{2,0,1:T(4,128)(2,1)S(1)}, bf16[4,3,8192]{2,0,1:T(4,128)(2,1)}, u32[]{:S(2)}) copy-start(bf16[4,3,8192]{2,0,1:T(4,128)(2,1)} %param.9) | copy-start | bytes 589828
